TPU v7x, 128 devices: a whole 4x4x4 slice. The times are simulated.
128 devices in a mesh: gx: 8 (over z, core), gy: 16 (over y, x).
Axes of the slice: x: 4, y: 4, z: 4, core: 2. Of those that a mesh axis runs over, the one named last changes fastest.
Arguments:
- token_ids: int32 [8, 64], replicated, may hold values from 0 to 65535
- cache_lengths: int32 [64], P('gy'), may hold values from 512 to 8192, as said below
- embed_table: bfloat16 [65536, 8192], P('gx', 'gy'), may hold values from -120 to 120
- norm_gain: bfloat16 [8192], P('gy'), may hold values from 0.099609375 to 1.8984375
- qkv_weight: bfloat16 [8192, 10240], P('gy', 'gx'), may hold values from -0.0625 to 0.0625
- key_cache: bfloat16 [64, 8192, 1024], P('gy', None, 'gx'), may hold values from -80 to 80
- value_cache: bfloat16 [64, 8192, 1024], P('gy', None, 'gx'), may hold values from -6 to 6
- out_weight: bfloat16 [8192, 8192], P('gx', 'gy'), may hold values from -0.5 to 0.5
Outputs:
- attn_out: bfloat16 [8, 64, 8192], P(None, 'gx', 'gy')
- new_kv: bfloat16 [2, 8, 64, 1024], P(None, None, 'gy', 'gx')
Inputs may be any that keep to these rules, and one draw needn't show every extreme that they name: `cache_lengths`: at least 512; one row of every draw holds exactly 8192.
All inputs are finite; a program needn't handle non-finite values.
Results may differ from a plain program's by a relative error of at most 0.012.
Values may be sent and summed in bfloat16 or wider, within the bound.
A program may use at most 128 MiB of HBM per device.

v0:
```python
import jax
import jax.numpy as jnp
from jax import lax
from jax.sharding import PartitionSpec as P

D = 8192
HD = 128
GROUP = 8


THETA = 500000.0
EPS = 1e-05
MASKED = -1e30


def rotate(field, positions):
    half_width = field.shape[-1] // 2
    inverse_freq = jnp.power(
        jnp.float32(THETA), -jnp.arange(half_width, dtype=jnp.float32) * (2.0 / field.shape[-1])
    )
    angles = positions[..., None].astype(jnp.float32) * inverse_freq
    front_half = field[..., :half_width]
    back_half = field[..., half_width:]
    cosine = jnp.cos(angles)
    sine = jnp.sin(angles)
    return jnp.concatenate(
        [front_half * cosine - back_half * sine, back_half * cosine + front_half * sine], -1
    )


def body(
    token_ids, cache_lengths, embed_table, norm_gain, qkv_weight, key_cache, value_cache, out_weight
):
    row_dev = cache_lengths.shape[0]
    heads_dev = key_cache.shape[2] // HD
    vocab_dev = embed_table.shape[0]
    context = key_cache.shape[1]
    block_steps = token_ids.shape[0]
    vocab_start = lax.axis_index("gx") * vocab_dev
    cache_keys = key_cache.reshape(row_dev, context, heads_dev, HD)
    cache_values = value_cache.reshape(row_dev, context, heads_dev, HD)
    valid = jnp.arange(context, dtype=jnp.int32)[None, :] < cache_lengths[:, None]
    offset_ids = jnp.transpose(token_ids) - vocab_start
    inside = (offset_ids >= 0) & (offset_ids < vocab_dev)
    picked = embed_table[jnp.clip(offset_ids, 0, vocab_dev - 1)].astype(jnp.float32)
    picked = jnp.where(inside[..., None], picked, 0.0)
    embedded = lax.psum(picked.astype(jnp.bfloat16), "gx").astype(jnp.float32)
    local_squares = jnp.sum(embedded * embedded, -1).reshape(-1)
    scaled = (embedded * norm_gain.astype(jnp.float32)).astype(jnp.bfloat16)
    flat_rows = scaled.reshape(-1, scaled.shape[-1])
    own_rows = row_dev * block_steps
    own_start = lax.axis_index("gy") * own_rows
    squares = lax.psum(local_squares, "gy")
    projected = lax.psum_scatter(
        jnp.dot(flat_rows, qkv_weight, preferred_element_type=jnp.float32),
        "gy",
        scatter_dimension=0,
        tiled=True,
    )
    own_squares = lax.dynamic_slice_in_dim(squares, own_start, own_rows, 0)
    inverse_rms = lax.rsqrt(own_squares / D + EPS)
    projected = projected * inverse_rms[:, None]
    projected = projected.reshape(row_dev, block_steps, heads_dev, GROUP + 2, HD)
    step_index = jnp.arange(block_steps, dtype=jnp.int32)
    positions = cache_lengths[:, None] + step_index[None, :]
    queries = (
        rotate(projected[:, :, :, :GROUP], positions[:, :, None, None]) * HD ** (-0.5)
    ).astype(jnp.bfloat16)
    keys_new = rotate(projected[:, :, :, GROUP], positions[:, :, None]).astype(jnp.bfloat16)
    values_new = projected[:, :, :, GROUP + 1].astype(jnp.bfloat16)
    cache_scores = jnp.einsum(
        "rthgd,rphd->rhgtp", queries, cache_keys, preferred_element_type=jnp.float32
    )
    cache_scores = jnp.where(valid[:, None, None, None, :], cache_scores, MASKED)
    fresh_scores = jnp.einsum(
        "rthgd,ruhd->rhgtu", queries, keys_new, preferred_element_type=jnp.float32
    )
    allowed = step_index[None, :] <= step_index[:, None]
    fresh_scores = jnp.where(allowed, fresh_scores, MASKED)
    largest = jnp.maximum(jnp.max(cache_scores, -1), jnp.max(fresh_scores, -1))[..., None]
    cache_exp = jnp.exp(cache_scores - largest)
    fresh_exp = jnp.exp(fresh_scores - largest)
    denominator = (jnp.sum(cache_exp, -1) + jnp.sum(fresh_exp, -1))[..., None]
    cache_weights = (cache_exp / denominator).astype(jnp.bfloat16)
    fresh_weights = (fresh_exp / denominator).astype(jnp.bfloat16)
    attended = jnp.einsum(
        "rhgtp,rphd->trhgd", cache_weights, cache_values, preferred_element_type=jnp.float32
    )
    attended = attended + jnp.einsum(
        "rhgtu,ruhd->trhgd", fresh_weights, values_new, preferred_element_type=jnp.float32
    )
    attended = attended.astype(jnp.bfloat16).reshape(block_steps, row_dev, heads_dev * GROUP * HD)
    partial_value = jnp.einsum(
        "tnf,fc->tnc",
        lax.all_gather(attended, "gy", axis=1, tiled=True),
        out_weight,
        preferred_element_type=jnp.float32,
    )
    attn_out = lax.psum_scatter(partial_value, "gx", scatter_dimension=1, tiled=True).astype(
        jnp.bfloat16
    )
    new_kv = jnp.stack(
        [
            jnp.transpose(keys_new, (1, 0, 2, 3)).reshape(block_steps, row_dev, heads_dev * HD),
            jnp.transpose(values_new, (1, 0, 2, 3)).reshape(block_steps, row_dev, heads_dev * HD),
        ]
    )
    return (attn_out, new_kv)


def solution(mesh):
    in_specs = (
        P(),
        P("gy"),
        P("gx", "gy"),
        P("gy"),
        P("gy", "gx"),
        P("gy", None, "gx"),
        P("gy", None, "gx"),
        P("gx", "gy"),
    )
    out_specs = (P(None, "gx", "gy"), P(None, None, "gy", "gx"))
    return jax.shard_map(body, mesh=mesh, in_specs=in_specs, out_specs=out_specs, check_vma=False)
```

profile of v0, /device:TPU:1, one launch (start us, length us, event | category | flops | bytes accessed | tf_op | source)
XLA Modules:
  0.0 253.0 jit_solution(15926817422045633689)
XLA Ops:
  7.2 0.0 copy-start
  7.2 0.0 copy-start.2
  7.2 0.0 all-reduce.2.cloned.1.call-start
  7.2 0.8 and_bitcast_fusion
  8.0 0.7 compare_select_fusion
  8.7 0.1 copy.28
  8.8 0.1 copy.29
  8.9 0.1 reshape.249
  9.0 6.4 %gather_fusion = bf16[512,512]{1,0:T(8,128)(2,1)S(1)} fusion(bf16[8192,512]{1,0:T(8,128)(2,1)} %param.10, s32[1024]{0:T(1024)S(1)} %pad_clamp_fusion), kind=kCustom, calls=%fused_computation | custom fusion | bytes 1050624 | tf_op jit(solution)/shard_map/gather | solution.py:45
  15.5 1.0 fusion.18
  16.4 0.0 all-reduce.2.cloned.1.call-update
  16.5 0.0 reduce-scatter.3.cloned.1.call-start
  16.5 0.7 convert_element_type.85
  17.2 61.5 %all-reduce.2.cloned.1.call-done = bf16[64,8,512]{2,1,0:T(8,128)(2,1)} async-done(((bf16[64,8,512]{2,1,0:T(8,128)(2,1)}), bf16[64,8,512]{2,1,0:T(8,128)(2,1)}) %all-reduce.2.cloned.1.call-update) | async-done | bytes 524304 | tf_op jit(solution)/shard_map/psum | solution.py:47
  78.7 0.0 copy-done
  78.7 0.0 copy-start.1
  78.7 3.5 %fusion.23 = f32[512,1280]{1,0:T(8,128)} fusion(bf16[512,1280]{1,0:T(8,128)(2,1)S(1)} %copy-done, bf16[64,8,512]{2,1,0:T(8,128)(2,1)} %all-reduce.2.cloned.1.call-done, f32[512]{0:T(512)S(1)} %convert_element_type.85), kind=kOutput, calls=%fused_computation.28 | convolution fusion | flops 671875072 | bytes 4458496 | tf_op jit(solution)/shard_map/dot_general | solution.py:55
  82.2 0.0 reduce-scatter.3.cloned.1.call-update
  82.2 0.0 all-gather.2.cloned.1.call-start
  82.3 0.0 copy-done.2
  82.3 0.1 add_convert_fusion
  82.4 0.1 multiply_cosine_fusion.1
  82.5 0.1 iota_compare_fusion
  82.6 0.0 copy-done.1
  82.7 0.2 fusion.17
  82.8 0.1 reshape.242
  82.9 33.3 %psum.15 = f32[512]{0:T(512)S(1)} all-reduce(f32[512]{0:T(512)S(1)} %reshape.242), channel_id=1, replica_groups=mesh['gx'=8,'gy'=16] {'gy'}, use_global_device_ids=true, to_apply=%region_3.4 | all-reduce | flops 512 | bytes 4096 | tf_op jit(solution)/shard_map/psum | solution.py:53
  116.2 0.1 add_rsqrt_fusion
  116.3 40.7 %reduce-scatter.3.cloned.1.call-done = f32[32,1280]{1,0:T(8,128)} async-done(((f32[512,1280]{1,0:T(8,128)}), f32[32,1280]{1,0:T(8,128)}) %reduce-scatter.3.cloned.1.call-update) | async-done | bytes 163856 | tf_op jit(solution)/shard_map/reduce_scatter | solution.py:54
  157.0 1.0 multiply_bitcast_fusion
  158.0 0.1 fusion.45
  158.1 0.1 fusion.35
  158.2 0.1 subtract_bitcast_fusion
  158.3 0.0 slice-start
  158.3 0.1 fusion.26
  158.4 0.0 slice-start.1
  158.4 6.6 %fusion.46 = (f32[4,8,8]{1,2,0:T(8,128)S(1)}, f32[4,1,8,8,8192]{4,2,3,0,1:T(8,128)S(1)}) fusion(bf16[4,8,8,128]{3,2,1,0:T(8,128)(2,1)S(1)} %fusion.26, bf16[4,8192,128]{2,1,0:T(8,128)(2,1)} %param.13, pred[4,8192]{1,0:T(4,128)(4,1)S(1)} %iota_compare_fusion), kind=kOutput, calls=%fused_computation.72 | convolution fusion | flops 541064960 | bytes 16876544 | tf_op jit(solution)/shard_map/rthgd,rphd->rhgtp/dot_general | solution.py:71
  165.0 0.4 fusion.47
  165.5 0.1 fusion.27
  165.6 1.3 fusion.5
  166.9 0.0 slice-done
  166.9 0.0 slice-done.1
  166.9 0.0 copy-start.3
  167.0 1.8 fusion.8
  168.7 0.2 fusion.15
  169.0 0.7 reshape.246
  169.6 0.0 all-gather.2.cloned.1.call-update
  169.7 0.0 reduce-scatter.5.cloned.1.call-start
  169.7 42.2 %all-gather.2.cloned.1.call-done = bf16[8,64,1024]{2,0,1:T(8,128)(2,1)} async-done(((bf16[8,4,1024]{2,0,1:T(8,128)(2,1)}), bf16[8,64,1024]{2,0,1:T(8,128)(2,1)}) %all-gather.2.cloned.1.call-update) | async-done | bytes 1048592 | tf_op jit(solution)/shard_map/all_gather | solution.py:95
  211.9 0.0 copy-done.3
  211.9 3.0 %fusion.19 = f32[8,64,512]{2,1,0:T(8,128)} fusion(bf16[1024,512]{1,0:T(8,128)(2,1)S(1)} %copy-done.3, bf16[8,64,1024]{2,0,1:T(8,128)(2,1)} %all-gather.2.cloned.1.call-done), kind=kOutput, calls=%fused_computation.24 | convolution fusion | flops 536870912 | bytes 3145728 | tf_op jit(solution)/shard_map/tnf,fc->tnc/dot_general | solution.py:93
  214.9 0.0 reduce-scatter.5.cloned.1.call-update
  214.9 0.1 maximum_bitcast_fusion.2
  215.0 0.6 copy.37
  215.6 29.3 %reduce-scatter.5.cloned.1.call-done = f32[8,8,512]{2,1,0:T(8,128)} async-done(((f32[8,64,512]{2,1,0:T(8,128)}), f32[8,8,512]{2,1,0:T(8,128)}) %reduce-scatter.5.cloned.1.call-update) | async-done | bytes 131088 | tf_op jit(solution)/shard_map/reduce_scatter | solution.py:99
  244.9 1.5 convert_element_type.96
  (9 shorter events, 0.1 us)
Async XLA Ops:
  7.2 71.6 %copy-start = (bf16[512,1280]{1,0:T(8,128)(2,1)S(1)}, bf16[512,1280]{1,0:T(8,128)(2,1)}, u32[]{:S(2)}) copy-start(bf16[512,1280]{1,0:T(8,128)(2,1)} %param.12) | copy-start | bytes 3932164
  7.2 75.1 %copy-start.2 = (s32[4]{0:T(128)S(1)}, s32[4]{0:T(128)}, u32[]{:S(2)}) copy-start(s32[4]{0:T(128)} %param.9) | copy-start | bytes 52
  7.2 71.5 %all-reduce.2.cloned.1.call-start = ((), (), s32[]{:S(2)}) async-start(), calls=%async_computation.2 | async-start | bytes 1048576 | tf_op jit(solution)/shard_map/psum | solution.py:47
  16.5 140.5 %reduce-scatter.3.cloned.1.call-start = ((), (), s32[]{:S(2)}) async-start(), calls=%async_computation.3 | async-start | bytes 2785280 | tf_op jit(solution)/shard_map/reduce_scatter | solution.py:54
  78.7 3.9 %copy-start.1 = (bf16[64,8,512]{2,1,0:T(8,128)(2,1)S(1)}, bf16[64,8,512]{2,1,0:T(8,128)(2,1)}, u32[]{:S(2)}) copy-start(bf16[64,8,512]{2,1,0:T(8,128)(2,1)} %all-reduce.2.cloned.1.call-done) | copy-start | bytes 1572868
  82.2 129.7 %all-gather.2.cloned.1.call-start = ((), (), s32[]{:S(2)}) async-start(), calls=%async_computation.4 | async-start | bytes 1114112 | tf_op jit(solution)/shard_map/all_gather | solution.py:95
  158.3 8.6 %slice-start = ((s8[8388608]{0:T(1024)(128)(4,1)}), s8[4194304]{0:T(1024)(128)(4,1)S(1)}, s32[]{:S(2)}) async-start(s8[8388608]{0:T(1024)(128)(4,1)} %bitcast.111), calls=%async_computation.6 | async-start | bytes 8388608
  158.4 8.5 %slice-start.1 = ((s8[8388608]{0:T(1024)(128)(4,1)}), s8[4194304]{0:T(1024)(128)(4,1)S(1)}, s32[]{:S(2)}) async-start(s8[8388608]{0:T(1024)(128)(4,1)} %bitcast.111), calls=%async_computation.7 | async-start | bytes 8388608
  166.9 45.0 %copy-start.3 = (bf16[1024,512]{1,0:T(8,128)(2,1)S(1)}, bf16[1024,512]{1,0:T(8,128)(2,1)}, u32[]{:S(2)}) copy-start(bf16[1024,512]{1,0:T(8,128)(2,1)} %param.15) | copy-start | bytes 3145732
  169.7 75.2 %reduce-scatter.5.cloned.1.call-start = ((), (), s32[]{:S(2)}) async-start(), calls=%async_computation.5 | async-start | bytes 1179648 | tf_op jit(solution)/shard_map/reduce_scatter | solution.py:99
Sparse Core Ops, SparseCore 0:
  16.6 62.0 all-reduce.1
  82.4 74.5 reduce-scatter.2
  169.8 42.0 all-gather.1
  215.0 29.7 reduce-scatter.4
where the time goes:
time: 256 us; the launch traced here: 253 us
  waiting for transfers between devices  174 us (68%)
  blocking collectives  33.3 us (13%)
  matrix products  15.5 us (6%)
  between operations  14 us (5%)
  local copies, waits for them, and re-layouts  8.23 us (3%)
  other arithmetic  8.09 us (3%)
    psum x1, waiting for transfers between devices, body(): embedded = lax.psum(picked.astype(jnp.bfloat16), 'gx').astype(jnp.float32)  61.5 us
    all_gather x1, waiting for transfers between devices, body(): lax.all_gather(attended, 'gy', axis=1, tiled=True)  42.2 us
    reduce_scatter x1, waiting for transfers between devices, body(): lax.psum_scatter(jnp.dot(flat_rows, qkv_weight, preferred_element_type=jn...  40.7 us
    psum x1, blocking collectives, body(): squares = lax.psum(local_squares, 'gy')  33.3 us
    reduce_scatter x1, waiting for transfers between devices, body(): lax.psum_scatter(partial_value, 'gx', scatter_dimension=1, tiled=True)  29.3 us
    dot_general x1, matrix products, body(): jnp.einsum('rthgd,rphd->rhgtp', queries, cache_keys, preferred_element_ty...  6.61 us
    gather x1, local copies, waits for them, and re-layouts, body(): embed_table[jnp.clip(offset_ids, 0, vocab_dev - 1)].astype(jnp.float32)  6.45 us
  transfers between devices with their start and end apart: 4, of which 4 were waited for; matrix products, arithmetic and copies ran while one was open for 1% of the time, Pallas kernels for 0%

commit v1 on v0

v1 whole, which is shorter than its diff:
```python
import functools
import math

import jax
import jax.numpy as jnp
import numpy as np
from jax import lax
from jax.experimental import pallas as pl
from jax.experimental.pallas import tpu as pltpu
from jax.sharding import PartitionSpec as P

D = 8192
HD = 128
GROUP = 8
STEPS = 8
THETA = 500000.0
EPS = 1e-05
MASKED = -1e30
MESH = pl.DeviceIdType.MESH

NCH = 2
RPC = 2
TPD = RPC * STEPS
TOK = 16 * TPD
SL = TOK // 8
TBLK = 1024
PBLK = 1024
F32 = jnp.float32
BF16 = jnp.bfloat16


def iota(shape, dim):
    return lax.broadcasted_iota(jnp.int32, shape, dim)


def kernel(
    ids_ref, len_ref, gain_ref, freq_ref, table_hbm, wqkv_hbm, key_hbm, val_hbm, wout_hbm,
    out_ref, kv_ref,
    table, wqkv, wout, kbuf, vbuf, acc,
    picks, r1a, s1, r1b, eall, part, ra, sb, rb, sq, rsq, ag, part5, r5a, s5, r5b, fin, kvs,
    local_sem, table_sem, send_sem, recv_sem,
):
    gx = lax.axis_index("gx")
    gy = lax.axis_index("gy")
    z, core = gx // 2, gx % 2
    y, x = gy // 4, gy % 4

    def wrap(a, k):
        return (a + k) % 4

    def at_core():
        return (z * 2 + 1 - core, gy)

    def at_z(k):
        return (wrap(z, k) * 2 + core, gy)

    def at_y(k):
        return (gx, wrap(y, k) * 4 + x)

    def at_x(k):
        return (gx, y * 4 + wrap(x, k))

    counter = [0]
    sends = []

    def remote(src, dst, device):
        n = counter[0]
        counter[0] += 1
        copy = pltpu.make_async_remote_copy(
            src_ref=src, dst_ref=dst, send_sem=send_sem.at[n], recv_sem=recv_sem.at[n],
            device_id=device, device_id_type=MESH,
        )
        copy.start()
        sends.append(copy)
        return copy

    nblk = table.shape[0]
    table_copies = []
    for b in range(nblk):
        copy = pltpu.make_async_copy(
            table_hbm.at[pl.ds(b * TBLK, TBLK)], table.at[b], table_sem.at[b]
        )
        copy.start()
        table_copies.append(copy)
    load_w = pltpu.make_async_copy(wqkv_hbm, wqkv, local_sem.at[0])
    load_o = pltpu.make_async_copy(wout_hbm, wout, local_sem.at[1])
    load_w.start()
    load_kv = []
    for c in range(NCH):
        rows = pl.ds(c * RPC, RPC)
        load_kv.append((
            pltpu.make_async_copy(key_hbm.at[rows], kbuf.at[rows], local_sem.at[2 + 2 * c]),
            pltpu.make_async_copy(val_hbm.at[rows], vbuf.at[rows], local_sem.at[3 + 2 * c]),
        ))
        for copy in load_kv[c]:
            copy.start()
    load_o.start()

    barrier = pltpu.get_barrier_semaphore()
    partners = [at_core()]
    for k in (1, 2, 3):
        partners += [at_z(k), at_y(k), at_x(k)]
    for device in partners:
        pl.semaphore_signal(barrier, inc=1, device_id=device, device_id_type=MESH)

    ids = ids_ref[...]
    id_high = (ids >> 8).astype(F32).astype(BF16)
    id_low = (ids & 255).astype(F32).astype(BF16)

    def local_ids(c):
        token = iota((TOK, 64), 0)
        row = (token // TPD) * (NCH * RPC) + c * RPC + (token // STEPS) % RPC
        chosen = jnp.where(iota((TOK, 64), 1) == row, 1.0, 0.0).astype(BF16)
        contract = (((1,), (1,)), ((), ()))
        high = lax.dot_general(chosen, id_high, contract, preferred_element_type=F32)
        low = lax.dot_general(chosen, id_low, contract, preferred_element_type=F32)
        both = high * 256.0 + low
        mine = iota((TOK, STEPS), 1) == iota((TOK, STEPS), 0) % STEPS
        column = jnp.sum(jnp.where(mine, both, 0.0), axis=1, keepdims=True)
        return column.astype(jnp.int32) - gx * (nblk * TBLK)

    def gather(c, first):
        local = local_ids(c)
        for b in range(nblk):
            if first:
                table_copies[b].wait()
            hot = jnp.where(iota((TOK, TBLK), 1) == local - b * TBLK, 1.0, 0.0).astype(BF16)
            term = jnp.dot(hot, table[b], preferred_element_type=F32)
            if b == 0:
                acc[...] = term
            else:
                acc[...] += term
        picks[c] = acc[...].astype(BF16).reshape(picks.shape[1:])

    def send_1a(c):
        return remote(picks.at[c, :, 1 - core], r1a.at[c], at_core())

    def send_1b(c, copy):
        copy.wait_recv()
        s1[c] = picks[c, :, core] + r1a[c]
        return [remote(s1.at[c, wrap(z, k)], r1b.at[c, k - 1], at_z(k)) for k in (1, 2, 3)]

    def send_1c(c, copies):
        for copy in copies:
            copy.wait_recv()
        eall[c, z, core] = (s1[c, z] + r1b[c, 0]) + (r1b[c, 1] + r1b[c, 2])
        mine = eall.at[c, z, core]
        return (
            [remote(mine, mine, at_z(k)) for k in (1, 2, 3)],
            [remote(mine, mine, at_core())],
        )

    def send_1d(c, copies):
        across, over = copies
        for k, copy in zip((1, 2, 3), across):
            copy.wait_recv()
            block = eall.at[c, wrap(z, 4 - k), core]
            over.append(remote(block, block, at_core()))
        return over

    half = wqkv.shape[1] // 2

    def send_2a(c, copies):
        for copy in copies:
            copy.wait_recv()
        embedded = eall[c].reshape(TOK, eall.shape[-1]).astype(F32)
        scaled = (embedded * gain_ref[...].astype(F32)).astype(BF16)
        product = jnp.dot(scaled, wqkv[...], preferred_element_type=F32)
        part[c] = product.astype(BF16).reshape(part.shape[1:])
        out = []
        for k in (1, 2, 3):
            out.append(remote(
                part.at[c, :, wrap(x, k), :, pl.ds(0, half)], ra.at[c, 0, k - 1], at_x(k)
            ))
            out.append(remote(
                part.at[c, wrap(y, k), :, :, pl.ds(half, half)], ra.at[c, 1, k - 1], at_y(k)
            ))
        squares = embedded * embedded
        high = squares.astype(BF16)
        low = (squares - high.astype(F32)).astype(BF16)
        ones = jnp.ones((8, eall.shape[-1]), BF16)
        contract = (((1,), (1,)), ((), ()))
        total = lax.dot_general(ones, high, contract, preferred_element_type=F32)
        total = total + lax.dot_general(ones, low, contract, preferred_element_type=F32)
        sq[c, 0] = total[:1]
        for k in (1, 2, 3):
            out.append(remote(sq.at[c, 0], rsq.at[c, 0, k - 1], at_x(k)))
        return out

    def send_2b(c, copies):
        for copy in copies:
            copy.wait_recv()
        sq[c, 1] = (sq[c, 0] + rsq[c, 0, 0]) + (rsq[c, 0, 1] + rsq[c, 0, 2])
        out = []
        for h, own in ((0, part[c, :, x, :, pl.ds(0, half)]), (1, part[c, y, :, :, pl.ds(half, half)])):
            total = own.astype(F32)
            for k in range(3):
                total = total + ra[c, h, k].astype(F32)
            sb[c, h] = total.astype(BF16)
        for k in (1, 2, 3):
            out.append(remote(sb.at[c, 0, wrap(y, k)], rb.at[c, 0, k - 1], at_y(k)))
            out.append(remote(sb.at[c, 1, wrap(x, k)], rb.at[c, 1, k - 1], at_x(k)))
            out.append(remote(sq.at[c, 1], rsq.at[c, 1, k - 1], at_y(k)))
        return out

    def queries(c, copies):
        for copy in copies:
            copy.wait_recv()
        squares = (sq[c, 1] + rsq[c, 1, 0]) + (rsq[c, 1, 1] + rsq[c, 1, 2])
        place = iota((TPD, TOK), 1) == iota((TPD, TOK), 0) + gy * TPD
        column = jnp.sum(jnp.where(place, squares, 0.0), axis=1, keepdims=True)
        inverse_rms = lax.rsqrt(column / D + EPS)
        pieces = []
        for h, own in ((0, sb[c, 0, y]), (1, sb[c, 1, x])):
            total = own.astype(F32)
            for k in range(3):
                total = total + rb[c, h, k].astype(F32)
            pieces.append(total)
        projected = jnp.concatenate(pieces, axis=1) * inverse_rms
        sub = iota((TPD, 1), 0)
        length = jnp.where(sub < STEPS, len_ref[c * RPC], len_ref[c * RPC + 1])
        position = (length + sub % STEPS).astype(F32)
        angle = position * freq_ref[...]
        cosine = jnp.cos(angle)
        sine = jnp.sin(angle)
        sine = jnp.where(iota((TPD, HD), 1) < HD // 2, -sine, sine)

        def rotate(g):
            field = projected[:, g * HD : (g + 1) * HD]
            return field * cosine + pltpu.roll(field, HD // 2, 1) * sine

        heads = [rotate(g) * HD ** (-0.5) for g in range(GROUP)]
        new_key = rotate(GROUP).astype(BF16)
        new_value = projected[:, (GROUP + 1) * HD :].astype(BF16)
        kvs[pl.ds(c * TPD, TPD)] = jnp.concatenate([new_key, new_value], axis=1)
        rows = [
            jnp.concatenate([head[r * STEPS : (r + 1) * STEPS] for head in heads], axis=0)
            for r in range(RPC)
        ]
        return rows, new_key, new_value

    nq = GROUP * STEPS

    def attention_start(rows, new_key, new_value):
        plain = jnp.concatenate(rows, axis=0).astype(BF16)
        nothing = jnp.zeros_like(rows[0])
        paired = jnp.concatenate(
            [
                jnp.concatenate([rows[0], nothing], axis=1),
                jnp.concatenate([nothing, rows[1]], axis=1),
            ],
            axis=0,
        ).astype(BF16)
        scores = lax.dot_general(
            plain, new_key, (((1,), (1,)), ((), ())), preferred_element_type=F32
        )
        query = iota(scores.shape, 0)
        entry = iota(scores.shape, 1)
        allowed = (entry // STEPS == query // nq) & (entry % STEPS <= query % STEPS)
        scores = jnp.where(allowed, scores, MASKED)
        largest = jnp.max(scores, axis=1, keepdims=True)
        weights = jnp.where(allowed, jnp.exp(scores - largest), 0.0)
        total = jnp.sum(weights, axis=1, keepdims=True)
        value = jnp.dot(weights.astype(BF16), new_value, preferred_element_type=F32)
        return paired, (largest, total, jnp.concatenate([value, value], axis=1))

    def attention_blocks(c, paired, state, first, last):
        r = c * RPC
        limits = (len_ref[r], len_ref[r + 1])

        def step(b, state):
            largest, total, value = state
            start = pl.multiple_of(b * PBLK, PBLK)
            where = pl.ds(start, PBLK)
            keys = jnp.concatenate([kbuf[r, where], kbuf[r + 1, where]], axis=1)
            values = jnp.concatenate([vbuf[r, where], vbuf[r + 1, where]], axis=1)
            scores = lax.dot_general(
                paired, keys, (((1,), (1,)), ((), ())), preferred_element_type=F32
            )
            place = iota((nq, PBLK), 1) + start
            scores = jnp.concatenate(
                [
                    jnp.where(place < limits[0], scores[:nq], MASKED),
                    jnp.where(place < limits[1], scores[nq:], MASKED),
                ],
                axis=0,
            )
            larger = jnp.maximum(largest, jnp.max(scores, axis=1, keepdims=True))
            shrink = jnp.exp(largest - larger)
            weights = jnp.exp(scores - larger)
            total = total * shrink + jnp.sum(weights, axis=1, keepdims=True)
            value = value * shrink + jnp.dot(
                weights.astype(BF16), values, preferred_element_type=F32
            )
            return larger, total, value

        return lax.fori_loop(first, last, step, state)

    def send_4a(c, state):
        _, total, value = state
        value = value / total
        columns = []
        for g in range(GROUP):
            columns.append(jnp.concatenate(
                [
                    value[r * nq + g * STEPS : r * nq + (g + 1) * STEPS, r * HD : (r + 1) * HD]
                    for r in range(RPC)
                ],
                axis=0,
            ))
        ag[c, 0, 0] = jnp.concatenate(columns, axis=1).astype(BF16)
        own = ag.at[c, 0, 0]
        out = ([], [])
        for k in (1, 2, 3):
            out[0].append(remote(own, ag.at[c, 0, k], at_x(k)))
            out[1].append(remote(own, ag.at[c, k, 0], at_y(k)))
        return out

    ahalf = wout.shape[0] // 2

    def send_4b(c, copies):
        along_x, along_y = copies
        out = []
        left, right = pl.ds(0, ahalf), pl.ds(ahalf, ahalf)
        others = pl.ds(1, 3)
        for copy in along_x:
            copy.wait_recv()
        for k in (1, 2, 3):
            out.append(remote(
                ag.at[c, 0, others, :, left], ag.at[c, k, others, :, left], at_y(k)
            ))
        for copy in along_y:
            copy.wait_recv()
        for k in (1, 2, 3):
            out.append(remote(
                ag.at[c, others, 0, :, right], ag.at[c, others, k, :, right], at_x(k)
            ))
        return out

    def send_5a(c, copies):
        for copy in copies:
            copy.wait_recv()
        everyone = ag[c].reshape(TOK, wout.shape[0])
        product = jnp.dot(everyone, wout[...], preferred_element_type=F32).astype(BF16)
        for ky in range(4):
            for kx in range(4):
                n = (ky * 4 + kx) * TPD
                place = wrap(x, 4 - kx)
                part5[c, wrap(y, 4 - ky), place // 2, place % 2] = product[n : n + TPD]
        return remote(part5.at[c, :, 1 - core], r5a.at[c], at_core())

    def send_5b(c, copy):
        copy.wait_recv()
        s5[c] = (part5[c, :, core].astype(F32) + r5a[c].astype(F32)).astype(BF16)
        return [remote(s5.at[c, wrap(z, k)], r5b.at[c, k - 1], at_z(k)) for k in (1, 2, 3)]

    def finish(c, copies):
        for copy in copies:
            copy.wait_recv()
        total = s5[c, z].astype(F32)
        for k in range(3):
            total = total + r5b[c, k].astype(F32)
        fin[pl.ds(c * SL, SL)] = total.astype(BF16).reshape(SL, total.shape[-1])

    gather(0, True)
    pl.semaphore_wait(barrier, len(partners))
    a1 = send_1a(0)
    gather(1, False)
    b1 = send_1a(1)
    a1 = send_1b(0, a1)
    b1 = send_1b(1, b1)
    a1 = send_1c(0, a1)
    b1 = send_1c(1, b1)
    a1 = send_1d(0, a1)
    load_w.wait()
    b1 = send_1d(1, b1)
    a2 = send_2a(0, a1)
    b2 = send_2a(1, b1)
    a2 = send_2b(0, a2)
    b2 = send_2b(1, b2)
    nb = kbuf.shape[1] // PBLK
    a_rows, a_key, a_value = queries(0, a2)
    for copy in load_kv[0]:
        copy.wait()
    paired, state = attention_start(a_rows, a_key, a_value)
    state = attention_blocks(0, paired, state, 0, nb)
    a4 = send_4a(0, state)
    b_rows, b_key, b_value = queries(1, b2)
    for copy in load_kv[1]:
        copy.wait()
    paired, state = attention_start(b_rows, b_key, b_value)
    state = attention_blocks(1, paired, state, 0, nb)
    b4 = send_4a(1, state)
    a4 = send_4b(0, a4)
    b4 = send_4b(1, b4)

    rows_dev = NCH * RPC
    size = rows_dev * STEPS
    order = iota((size, size), 0)
    source = (order % rows_dev) * STEPS + order // rows_dev
    perm = jnp.where(iota((size, size), 1) == source, 1.0, 0.0).astype(BF16)
    fresh = jnp.dot(perm, kvs[...], preferred_element_type=F32).astype(BF16)
    kv_ref[0] = fresh[:, :HD]
    kv_ref[1] = fresh[:, HD:]

    load_o.wait()
    a5 = send_5a(0, a4)
    a5 = send_5b(0, a5)
    b5 = send_5a(1, b4)
    b5 = send_5b(1, b5)
    finish(0, a5)
    finish(1, b5)

    size = NCH * SL
    order = iota((size, size), 0)
    step, row = order // 8, order % 8
    source = ((row // RPC) % NCH) * SL + (row // (RPC * NCH)) * TPD + (row % RPC) * STEPS + step
    perm = jnp.where(iota((size, size), 1) == source, 1.0, 0.0).astype(BF16)
    out_ref[...] = jnp.dot(perm, fin[...], preferred_element_type=F32).astype(BF16)

    for copy in sends:
        copy.wait_send()


COPIES = NCH * (1 + 3 + 3 + 4 + 9 + 9 + 6 + 6 + 1 + 3)


def body(
    token_ids, cache_lengths, embed_table, norm_gain, qkv_weight, key_cache, value_cache, out_weight
):
    vocab, feats = embed_table.shape
    cols = qkv_weight.shape[1]
    width, out_cols = out_weight.shape
    frequency = THETA ** (-np.arange(HD // 2, dtype=np.float64) * (2.0 / HD))
    frequency = np.concatenate([frequency, frequency]).astype(np.float32)[None, :]
    vmem = pl.BlockSpec(memory_space=pltpu.VMEM)
    hbm = pl.BlockSpec(memory_space=pl.ANY)
    smem = pl.BlockSpec(memory_space=pltpu.SMEM)
    dma = pltpu.SemaphoreType.DMA
    half = cols // 2
    out, kv = pl.pallas_call(
        kernel,
        out_shape=(
            jax.ShapeDtypeStruct((NCH * SL, out_cols), BF16),
            jax.ShapeDtypeStruct((2, NCH * TPD, HD), BF16),
        ),
        in_specs=[vmem, smem, vmem, vmem, hbm, hbm, hbm, hbm, hbm],
        out_specs=(vmem, vmem),
        scratch_shapes=[
            pltpu.VMEM((vocab // TBLK, TBLK, feats), BF16),
            pltpu.VMEM(qkv_weight.shape, BF16),
            pltpu.VMEM(out_weight.shape, BF16),
            pltpu.VMEM(key_cache.shape, BF16),
            pltpu.VMEM(value_cache.shape, BF16),
            pltpu.VMEM((TOK, feats), F32),
            pltpu.VMEM((NCH, 4, 2, SL, feats), BF16),
            pltpu.VMEM((NCH, 4, SL, feats), BF16),
            pltpu.VMEM((NCH, 4, SL, feats), BF16),
            pltpu.VMEM((NCH, 3, SL, feats), BF16),
            pltpu.VMEM((NCH, 4, 2, SL, feats), BF16),
            pltpu.VMEM((NCH, 4, 4, TPD, cols), BF16),
            pltpu.VMEM((NCH, 2, 3, 4, TPD, half), BF16),
            pltpu.VMEM((NCH, 2, 4, TPD, half), BF16),
            pltpu.VMEM((NCH, 2, 3, TPD, half), BF16),
            pltpu.VMEM((NCH, 2, 1, TOK), F32),
            pltpu.VMEM((NCH, 2, 3, 1, TOK), F32),
            pltpu.VMEM((NCH, 4, 4, TPD, width), BF16),
            pltpu.VMEM((NCH, 4, 2, 2, TPD, out_cols), BF16),
            pltpu.VMEM((NCH, 4, 2, TPD, out_cols), BF16),
            pltpu.VMEM((NCH, 4, 2, TPD, out_cols), BF16),
            pltpu.VMEM((NCH, 3, 2, TPD, out_cols), BF16),
            pltpu.VMEM((NCH * SL, out_cols), BF16),
            pltpu.VMEM((NCH * TPD, 2 * HD), BF16),
            dma((2 + 2 * NCH,)),
            dma((vocab // TBLK,)),
            dma((COPIES,)),
            dma((COPIES,)),
        ],
        compiler_params=pltpu.CompilerParams(
            collective_id=0, has_side_effects=True, vmem_limit_bytes=56 << 20
        ),
        cost_estimate=pl.CostEstimate(
            flops=8 * 10**9, bytes_accessed=30 * 10**6, transcendentals=2 * 10**6
        ),
        name="decode_block",
    )(
        token_ids, cache_lengths, norm_gain[None, :], jnp.asarray(frequency), embed_table,
        qkv_weight, key_cache, value_cache, out_weight,
    )
    return (
        out.reshape(STEPS, NCH * SL // STEPS, out_cols),
        kv.reshape(2, STEPS, NCH * RPC, HD),
    )


def solution(mesh):
    in_specs = (
        P(),
        P("gy"),
        P("gx", "gy"),
        P("gy"),
        P("gy", "gx"),
        P("gy", None, "gx"),
        P("gy", None, "gx"),
        P("gx", "gy"),
    )
    out_specs = (P(None, "gx", "gy"), P(None, None, "gy", "gx"))
    return jax.shard_map(body, mesh=mesh, in_specs=in_specs, out_specs=out_specs, check_vma=False)
```

time: 256 us -> 71.3 us (0.28); the launches traced: 253 us -> 71.1 us
  waiting for transfers between devices: 174 us -> 0 us
  Pallas kernels: 0 us -> 66.4 us
  blocking collectives: 33.3 us -> 0 us
  matrix products: 15.5 us -> 0 us
  between operations: 14 us -> 0.64 us
  other arithmetic: 8.09 us -> 0 us
  local copies, waits for them, and re-layouts: 8.23 us -> 4.06 us
    reduce_scatter x2 -> x0, waiting for transfers between devices: 69.9 us -> none  [the longest x1 40.7 us: body(): lax.psum_scatter(jnp.dot(flat_rows, qkv_weight, preferred_element_type=jn...]
    pallas_call x0 -> x1, Pallas kernels: none -> 66.4 us  [body(): pl.pallas_call(kernel, out_shape=(jax.ShapeDtypeStruct((NCH * SL, out_col...]
    psum x1 -> x0, waiting for transfers between devices: 61.5 us -> none  [body(): embedded = lax.psum(picked.astype(jnp.bfloat16), 'gx').astype(jnp.float32)]
    all_gather x1 -> x0, waiting for transfers between devices: 42.2 us -> none  [body(): lax.all_gather(attended, 'gy', axis=1, tiled=True)]
    psum x1 -> x0, blocking collectives: 33.3 us -> none  [body(): squares = lax.psum(local_squares, 'gy')]
    dot_general x6 -> x0, matrix products: 15.5 us -> none  [the longest x1 6.61 us: body(): jnp.einsum('rthgd,rphd->rhgtp', queries, cache_keys, preferred_element_ty...]
    gather x1 -> x0, local copies, waits for them, and re-layouts: 6.45 us -> none  [body(): embed_table[jnp.clip(offset_ids, 0, vocab_dev - 1)].astype(jnp.float32)]
    convert_element_type x5 -> x0, other arithmetic: 3.38 us -> none  [the longest x1 1.54 us: body(): lax.psum_scatter(partial_value, 'gx', scatter_dimension=1, tiled=True)]
  transfers between devices with their start and end apart: 4 -> 0, of which waited for: 4 -> 0; matrix products, arithmetic and copies ran while one was open for 1% -> 0% of each run, Pallas kernels for 0% -> 0%
where the time goes in v1:
time: 71.3 us; the launch traced here: 71.1 us
  Pallas kernels  66.4 us (93%)
  local copies, waits for them, and re-layouts  4.06 us (6%)
    pallas_call x1, Pallas kernels, body(): pl.pallas_call(kernel, out_shape=(jax.ShapeDtypeStruct((NCH * SL, out_col...  66.4 us
    unnamed x2, local copies, waits for them, and re-layouts  2.8 us

profile of v1, /device:TPU:1, one launch (start us, length us, event | category | flops | bytes accessed | tf_op | source)
XLA Modules:
  0.0 71.1 jit_solution(11039089058882558810)
XLA Ops:
  0.6 1.3 %broadcast_in_dim.3.gain_ref = bf16[1,512]{1,0:T(2,128)(2,1)} reshape(bf16[512]{0:T(512)(128)(2,1)} %param.12) | data formatting | bytes 2048 | tf_op jit(solution)/shard_map/broadcast_in_dim | solution.py:487
  1.9 66.4 %decode_block.1 = (bf16[64,512]{1,0:T(8,128)(2,1)}, bf16[2,32,128]{2,1,0:T(8,128)(2,1)}) custom-call(s32[8,64]{1,0:T(8,128)} %ids_ref.1, s32[4]{0:T(128)} %len_ref.1, bf16[1,512]{1,0:T(2,128)(2,1)} %broadcast_in_dim.3.gain_ref, f32[1,128]{1,0:T(1,128)} %constant.2.clone.freq_ref, bf16[8192,512]{1,0:T(8,128)(2,1)} %table_hbm.1, bf16[512,1280]{1,0:T(8,128)(2,1)} %wqkv_hbm.1, ...), custom_call_target="tpu_custom_call" | custom-call | flops 8000000000 | bytes 30000000 | tf_op jit(solution)/shard_map/decode_block/pallas_call | solution.py:441
  68.3 1.5 %copy.13 = bf16[8,8,512]{2,1,0:T(8,128)(2,1)} copy(bf16[8,8,512]{2,1,0:T(8,128)(2,1)} %bitcast.2) | data formatting | bytes 131072
  69.7 1.3 %copy.14 = bf16[2,8,4,128]{3,2,1,0:T(4,128)(2,1)} copy(bf16[2,8,4,128]{3,2,1,0:T(4,128)(2,1)} %bitcast.3) | data formatting | bytes 32768

commit v2 on v1

--- a/solution.py
+++ b/solution.py
@@ -24,7 +24,7 @@
 TOK = 16 * TPD
 SL = TOK // 8
 TBLK = 1024
-PBLK = 1024
+PBLK = 2048
 F32 = jnp.float32
 BF16 = jnp.bfloat16
 
@@ -35,9 +35,9 @@
 
 def kernel(
     ids_ref, len_ref, gain_ref, freq_ref, table_hbm, wqkv_hbm, key_hbm, val_hbm, wout_hbm,
-    out_ref, kv_ref,
+    fin, kvs,
     table, wqkv, wout, kbuf, vbuf, acc,
-    picks, r1a, s1, r1b, eall, part, ra, sb, rb, sq, rsq, ag, part5, r5a, s5, r5b, fin, kvs,
+    picks, r1a, s1, r1b, eall, part, ra, sb, rb, sq, rsq, scores, ag, part5, r5a, s5, r5b,
     local_sem, table_sem, send_sem, recv_sem,
 ):
     gx = lax.axis_index("gx")
@@ -84,7 +84,6 @@
         table_copies.append(copy)
     load_w = pltpu.make_async_copy(wqkv_hbm, wqkv, local_sem.at[0])
     load_o = pltpu.make_async_copy(wout_hbm, wout, local_sem.at[1])
-    load_w.start()
     load_kv = []
     for c in range(NCH):
         rows = pl.ds(c * RPC, RPC)
@@ -92,9 +91,13 @@
             pltpu.make_async_copy(key_hbm.at[rows], kbuf.at[rows], local_sem.at[2 + 2 * c]),
             pltpu.make_async_copy(val_hbm.at[rows], vbuf.at[rows], local_sem.at[3 + 2 * c]),
         ))
-        for copy in load_kv[c]:
-            copy.start()
-    load_o.start()
+
+    def start_loads():
+        load_w.start()
+        for pair in load_kv:
+            for copy in pair:
+                copy.start()
+        load_o.start()
 
     barrier = pltpu.get_barrier_semaphore()
     partners = [at_core()]
@@ -124,6 +127,8 @@
         for b in range(nblk):
             if first:
                 table_copies[b].wait()
+                if b == nblk - 1:
+                    start_loads()
             hot = jnp.where(iota((TOK, TBLK), 1) == local - b * TBLK, 1.0, 0.0).astype(BF16)
             term = jnp.dot(hot, table[b], preferred_element_type=F32)
             if b == 0:
@@ -164,7 +169,7 @@
         for copy in copies:
             copy.wait_recv()
         embedded = eall[c].reshape(TOK, eall.shape[-1]).astype(F32)
-        scaled = (embedded * gain_ref[...].astype(F32)).astype(BF16)
+        scaled = (embedded * gain_ref[...].astype(F32)[None, :]).astype(BF16)
         product = jnp.dot(scaled, wqkv[...], preferred_element_type=F32)
         part[c] = product.astype(BF16).reshape(part.shape[1:])
         out = []
@@ -241,7 +246,7 @@
 
     nq = GROUP * STEPS
 
-    def attention_start(rows, new_key, new_value):
+    def attention_scores(c, rows, new_key):
         plain = jnp.concatenate(rows, axis=0).astype(BF16)
         nothing = jnp.zeros_like(rows[0])
         paired = jnp.concatenate(
@@ -251,53 +256,73 @@
             ],
             axis=0,
         ).astype(BF16)
-        scores = lax.dot_general(
+        fresh = lax.dot_general(
             plain, new_key, (((1,), (1,)), ((), ())), preferred_element_type=F32
         )
-        query = iota(scores.shape, 0)
-        entry = iota(scores.shape, 1)
+        query = iota(fresh.shape, 0)
+        entry = iota(fresh.shape, 1)
         allowed = (entry // STEPS == query // nq) & (entry % STEPS <= query % STEPS)
-        scores = jnp.where(allowed, scores, MASKED)
-        largest = jnp.max(scores, axis=1, keepdims=True)
-        weights = jnp.where(allowed, jnp.exp(scores - largest), 0.0)
-        total = jnp.sum(weights, axis=1, keepdims=True)
-        value = jnp.dot(weights.astype(BF16), new_value, preferred_element_type=F32)
-        return paired, (largest, total, jnp.concatenate([value, value], axis=1))
-
-    def attention_blocks(c, paired, state, first, last):
+        fresh = jnp.where(allowed, fresh, MASKED)
         r = c * RPC
         limits = (len_ref[r], len_ref[r + 1])
 
-        def step(b, state):
-            largest, total, value = state
+        def step(b, largest):
             start = pl.multiple_of(b * PBLK, PBLK)
             where = pl.ds(start, PBLK)
             keys = jnp.concatenate([kbuf[r, where], kbuf[r + 1, where]], axis=1)
-            values = jnp.concatenate([vbuf[r, where], vbuf[r + 1, where]], axis=1)
-            scores = lax.dot_general(
+            block = lax.dot_general(
                 paired, keys, (((1,), (1,)), ((), ())), preferred_element_type=F32
             )
             place = iota((nq, PBLK), 1) + start
-            scores = jnp.concatenate(
+            block = jnp.concatenate(
                 [
-                    jnp.where(place < limits[0], scores[:nq], MASKED),
-                    jnp.where(place < limits[1], scores[nq:], MASKED),
+                    jnp.where(place < limits[0], block[:nq], MASKED),
+                    jnp.where(place < limits[1], block[nq:], MASKED),
                 ],
                 axis=0,
             )
-            larger = jnp.maximum(largest, jnp.max(scores, axis=1, keepdims=True))
-            shrink = jnp.exp(largest - larger)
-            weights = jnp.exp(scores - larger)
-            total = total * shrink + jnp.sum(weights, axis=1, keepdims=True)
-            value = value * shrink + jnp.dot(
-                weights.astype(BF16), values, preferred_element_type=F32
-            )
-            return larger, total, value
-
-        return lax.fori_loop(first, last, step, state)
+            scores[b] = block
+            for n in range(0, PBLK, HD):
+                largest = jnp.maximum(largest, block[:, n : n + HD])
+            return largest
+
+        largest = lax.fori_loop(
+            0, scores.shape[0], step, jnp.full((RPC * nq, HD), MASKED, F32), unroll=2
+        )
+        largest = jnp.maximum(
+            jnp.max(largest, axis=1, keepdims=True), jnp.max(fresh, axis=1, keepdims=True)
+        )
+        return allowed, fresh, largest
+
+    def attention_values(c, state, new_value):
+        allowed, fresh, largest = state
+        r = c * RPC
+        fresh = jnp.where(allowed, jnp.exp(fresh - largest), 0.0)
+        fresh_total = jnp.sum(fresh, axis=1, keepdims=True)
+        value = jnp.dot(fresh.astype(BF16), new_value, preferred_element_type=F32)
+        level = jnp.broadcast_to(largest, (RPC * nq, HD))
+
+        def step(b, state):
+            total, value = state
+            where = pl.ds(pl.multiple_of(b * PBLK, PBLK), PBLK)
+            pieces = []
+            for n in range(0, PBLK, HD):
+                piece = jnp.exp(scores[b, :, n : n + HD] - level)
+                total = total + piece
+                pieces.append(piece.astype(BF16))
+            weights = jnp.concatenate(pieces, axis=1)
+            values = jnp.concatenate([vbuf[r, where], vbuf[r + 1, where]], axis=1)
+            value = value + jnp.dot(weights, values, preferred_element_type=F32)
+            return total, value
+
+        total, value = lax.fori_loop(
+            0, scores.shape[0], step,
+            (jnp.zeros((RPC * nq, HD), F32), jnp.concatenate([value, value], axis=1)), unroll=2,
+        )
+        return jnp.sum(total, axis=1, keepdims=True) + fresh_total, value
 
     def send_4a(c, state):
-        _, total, value = state
+        total, value = state
         value = value / total
         columns = []
         for g in range(GROUP):
@@ -378,22 +403,32 @@
     b2 = send_2a(1, b1)
     a2 = send_2b(0, a2)
     b2 = send_2b(1, b2)
-    nb = kbuf.shape[1] // PBLK
     a_rows, a_key, a_value = queries(0, a2)
     for copy in load_kv[0]:
         copy.wait()
-    paired, state = attention_start(a_rows, a_key, a_value)
-    state = attention_blocks(0, paired, state, 0, nb)
-    a4 = send_4a(0, state)
+    state = attention_scores(0, a_rows, a_key)
+    a4 = send_4a(0, attention_values(0, state, a_value))
     b_rows, b_key, b_value = queries(1, b2)
     for copy in load_kv[1]:
         copy.wait()
-    paired, state = attention_start(b_rows, b_key, b_value)
-    state = attention_blocks(1, paired, state, 0, nb)
-    b4 = send_4a(1, state)
+    state = attention_scores(1, b_rows, b_key)
     a4 = send_4b(0, a4)
+    b4 = send_4a(1, attention_values(1, state, b_value))
     b4 = send_4b(1, b4)
 
+    load_o.wait()
+    a5 = send_5a(0, a4)
+    a5 = send_5b(0, a5)
+    b5 = send_5a(1, b4)
+    b5 = send_5b(1, b5)
+    finish(0, a5)
+    finish(1, b5)
+
+    for copy in sends:
+        copy.wait_send()
+
+
+def order_outputs(fin, kvs, out_ref, kv_ref):
     rows_dev = NCH * RPC
     size = rows_dev * STEPS
     order = iota((size, size), 0)
@@ -403,13 +438,6 @@
     kv_ref[0] = fresh[:, :HD]
     kv_ref[1] = fresh[:, HD:]
 
-    load_o.wait()
-    a5 = send_5a(0, a4)
-    a5 = send_5b(0, a5)
-    b5 = send_5a(1, b4)
-    b5 = send_5b(1, b5)
-    finish(0, a5)
-    finish(1, b5)
 
     size = NCH * SL
     order = iota((size, size), 0)
@@ -417,9 +445,6 @@
     source = ((row // RPC) % NCH) * SL + (row // (RPC * NCH)) * TPD + (row % RPC) * STEPS + step
     perm = jnp.where(iota((size, size), 1) == source, 1.0, 0.0).astype(BF16)
     out_ref[...] = jnp.dot(perm, fin[...], preferred_element_type=F32).astype(BF16)
-
-    for copy in sends:
-        copy.wait_send()
 
 
 COPIES = NCH * (1 + 3 + 3 + 4 + 9 + 9 + 6 + 6 + 1 + 3)
@@ -438,11 +463,11 @@
     smem = pl.BlockSpec(memory_space=pltpu.SMEM)
     dma = pltpu.SemaphoreType.DMA
     half = cols // 2
-    out, kv = pl.pallas_call(
+    fin, kvs = pl.pallas_call(
         kernel,
         out_shape=(
             jax.ShapeDtypeStruct((NCH * SL, out_cols), BF16),
-            jax.ShapeDtypeStruct((2, NCH * TPD, HD), BF16),
+            jax.ShapeDtypeStruct((NCH * TPD, 2 * HD), BF16),
         ),
         in_specs=[vmem, smem, vmem, vmem, hbm, hbm, hbm, hbm, hbm],
         out_specs=(vmem, vmem),
@@ -464,13 +489,12 @@
             pltpu.VMEM((NCH, 2, 3, TPD, half), BF16),
             pltpu.VMEM((NCH, 2, 1, TOK), F32),
             pltpu.VMEM((NCH, 2, 3, 1, TOK), F32),
+            pltpu.VMEM((key_cache.shape[1] // PBLK, RPC * GROUP * STEPS, PBLK), F32),
             pltpu.VMEM((NCH, 4, 4, TPD, width), BF16),
             pltpu.VMEM((NCH, 4, 2, 2, TPD, out_cols), BF16),
             pltpu.VMEM((NCH, 4, 2, TPD, out_cols), BF16),
             pltpu.VMEM((NCH, 4, 2, TPD, out_cols), BF16),
             pltpu.VMEM((NCH, 3, 2, TPD, out_cols), BF16),
-            pltpu.VMEM((NCH * SL, out_cols), BF16),
-            pltpu.VMEM((NCH * TPD, 2 * HD), BF16),
             dma((2 + 2 * NCH,)),
             dma((vocab // TBLK,)),
             dma((COPIES,)),
@@ -484,9 +508,19 @@
         ),
         name="decode_block",
     )(
-        token_ids, cache_lengths, norm_gain[None, :], jnp.asarray(frequency), embed_table,
+        token_ids, cache_lengths, norm_gain, jnp.asarray(frequency), embed_table,
         qkv_weight, key_cache, value_cache, out_weight,
     )
+    out, kv = pl.pallas_call(
+        order_outputs,
+        out_shape=(
+            jax.ShapeDtypeStruct((NCH * SL, out_cols), BF16),
+            jax.ShapeDtypeStruct((2, NCH * TPD, HD), BF16),
+        ),
+        in_specs=[vmem, vmem],
+        out_specs=(vmem, vmem),
+        name="order_outputs",
+    )(fin, kvs)
     return (
         out.reshape(STEPS, NCH * SL // STEPS, out_cols),
         kv.reshape(2, STEPS, NCH * RPC, HD),

time: 71.3 us -> 61.5 us (0.86)
  Pallas kernels: 66.4 us -> 60.7 us
  local copies, waits for them, and re-layouts: 4.06 us -> 0 us
    pallas_call x1, Pallas kernels: 66.4 us -> 59 us  [body(): pl.pallas_call(kernel, out_shape=(jax.ShapeDtypeStruct((NCH * SL, out_col...]
    unnamed x2 -> x0, local copies, waits for them, and re-layouts: 2.8 us -> none
    pallas_call x0 -> x1, Pallas kernels: none -> 1.64 us  [body(): pl.pallas_call(order_outputs, out_shape=(jax.ShapeDtypeStruct((NCH * SL,...]
    broadcast_in_dim x1 -> x0, local copies, waits for them, and re-layouts: 1.26 us -> none  [body(): norm_gain[None, :]]
where the time goes in v2:
time: 61.5 us; the launch traced here: 61.3 us
  Pallas kernels  60.7 us (99%)
  between operations  0.64 us (1%)
    pallas_call x1, Pallas kernels, body(): pl.pallas_call(kernel, out_shape=(jax.ShapeDtypeStruct((NCH * SL, out_col...  59 us
    pallas_call x1, Pallas kernels, body(): pl.pallas_call(order_outputs, out_shape=(jax.ShapeDtypeStruct((NCH * SL,...  1.64 us

profile of v2, /device:TPU:1, one launch (start us, length us, event | category | flops | bytes accessed | tf_op | source)
XLA Modules:
  0.0 61.3 jit_solution(9878237905270722339)
XLA Ops:
  0.6 59.0 %decode_block.1 = (bf16[64,512]{1,0:T(8,128)(2,1)}, bf16[32,256]{1,0:T(8,128)(2,1)}) custom-call(s32[8,64]{1,0:T(8,128)} %ids_ref.1, s32[4]{0:T(128)} %len_ref.1, bf16[512]{0:T(512)(128)(2,1)} %gain_ref.1, f32[1,128]{1,0:T(1,128)} %constant.2.clone.freq_ref, bf16[8192,512]{1,0:T(8,128)(2,1)} %table_hbm.1, bf16[512,1280]{1,0:T(8,128)(2,1)} %wqkv_hbm.1, ...), custom_call_target="tpu_custom_call" | custom-call | flops 8000000000 | bytes 30000000 | tf_op jit(solution)/shard_map/decode_block/pallas_call | solution.py:466
  59.7 1.6 %order_outputs.1 = (bf16[64,512]{1,0:T(8,128)(2,1)}, bf16[2,32,128]{2,1,0:T(8,128)(2,1)}) custom-call(bf16[64,512]{1,0:T(8,128)(2,1)} %get-tuple-element.6.fin, bf16[32,256]{1,0:T(8,128)(2,1)} %get-tuple-element.7.kvs), custom_call_target="tpu_custom_call" | custom-call | tf_op jit(solution)/shard_map/order_outputs/pallas_call | solution.py:514

commit v3 on v2

--- a/solution.py
+++ b/solution.py
@@ -23,8 +23,9 @@
 TPD = RPC * STEPS
 TOK = 16 * TPD
 SL = TOK // 8
-TBLK = 1024
-PBLK = 2048
+TBLK = 2048
+PBLK = 4096
+TURN = 1024
 F32 = jnp.float32
 BF16 = jnp.bfloat16
 
@@ -34,11 +35,11 @@
 
 
 def kernel(
-    ids_ref, len_ref, gain_ref, freq_ref, table_hbm, wqkv_hbm, key_hbm, val_hbm, wout_hbm,
+    len_ref, ids_hbm, gain_hbm, freq_hbm, table_hbm, wqkv_hbm, key_hbm, val_hbm, wout_hbm,
     fin, kvs,
-    table, wqkv, wout, kbuf, vbuf, acc,
+    ids_ref, gain_ref, freq_ref, table, wqkv, wout, kbuf, kturned, vbuf, acc,
     picks, r1a, s1, r1b, eall, part, ra, sb, rb, sq, rsq, scores, ag, part5, r5a, s5, r5b,
-    local_sem, table_sem, send_sem, recv_sem,
+    small_sem, local_sem, table_sem, send_sem, recv_sem,
 ):
     gx = lax.axis_index("gx")
     gy = lax.axis_index("gy")
@@ -74,6 +75,14 @@
         sends.append(copy)
         return copy
 
+    small = [
+        pltpu.make_async_copy(hbm, ref, small_sem.at[n])
+        for n, (hbm, ref) in enumerate(
+            ((ids_hbm, ids_ref), (gain_hbm, gain_ref), (freq_hbm, freq_ref))
+        )
+    ]
+    for copy in small:
+        copy.start()
     nblk = table.shape[0]
     table_copies = []
     for b in range(nblk):
@@ -106,6 +115,8 @@
     for device in partners:
         pl.semaphore_signal(barrier, inc=1, device_id=device, device_id_type=MESH)
 
+    for copy in small:
+        copy.wait()
     ids = ids_ref[...]
     id_high = (ids >> 8).astype(F32).astype(BF16)
     id_low = (ids & 255).astype(F32).astype(BF16)
@@ -122,20 +133,17 @@
         column = jnp.sum(jnp.where(mine, both, 0.0), axis=1, keepdims=True)
         return column.astype(jnp.int32) - gx * (nblk * TBLK)
 
-    def gather(c, first):
-        local = local_ids(c)
-        for b in range(nblk):
-            if first:
-                table_copies[b].wait()
-                if b == nblk - 1:
-                    start_loads()
-            hot = jnp.where(iota((TOK, TBLK), 1) == local - b * TBLK, 1.0, 0.0).astype(BF16)
-            term = jnp.dot(hot, table[b], preferred_element_type=F32)
-            if b == 0:
-                acc[...] = term
-            else:
-                acc[...] += term
-        picks[c] = acc[...].astype(BF16).reshape(picks.shape[1:])
+    local = [local_ids(c) for c in range(NCH)]
+
+    def gather(c, b):
+        hot = jnp.where(iota((TOK, TBLK), 1) == local[c] - b * TBLK, 1.0, 0.0).astype(BF16)
+        term = jnp.dot(hot, table[b], preferred_element_type=F32)
+        if b == 0:
+            acc[c] = term
+        elif b < nblk - 1:
+            acc[c] += term
+        else:
+            picks[c] = (acc[c] + term).astype(BF16).reshape(picks.shape[1:])
 
     def send_1a(c):
         return remote(picks.at[c, :, 1 - core], r1a.at[c], at_core())
@@ -170,16 +178,17 @@
             copy.wait_recv()
         embedded = eall[c].reshape(TOK, eall.shape[-1]).astype(F32)
         scaled = (embedded * gain_ref[...].astype(F32)[None, :]).astype(BF16)
-        product = jnp.dot(scaled, wqkv[...], preferred_element_type=F32)
-        part[c] = product.astype(BF16).reshape(part.shape[1:])
         out = []
-        for k in (1, 2, 3):
-            out.append(remote(
-                part.at[c, :, wrap(x, k), :, pl.ds(0, half)], ra.at[c, 0, k - 1], at_x(k)
-            ))
-            out.append(remote(
-                part.at[c, wrap(y, k), :, :, pl.ds(half, half)], ra.at[c, 1, k - 1], at_y(k)
-            ))
+        for h in range(2):
+            own = pl.ds(h * half, half)
+            product = jnp.dot(scaled, wqkv[:, own], preferred_element_type=F32)
+            part[c, :, :, :, own] = product.astype(BF16).reshape(4, 4, TPD, half)
+            for k in (1, 2, 3):
+                if h == 0:
+                    block, device = part.at[c, :, wrap(x, k), :, own], at_x(k)
+                else:
+                    block, device = part.at[c, wrap(y, k), :, :, own], at_y(k)
+                out.append(remote(block, ra.at[c, h, k - 1], device))
         squares = embedded * embedded
         high = squares.astype(BF16)
         low = (squares - high.astype(F32)).astype(BF16)
@@ -202,10 +211,12 @@
             for k in range(3):
                 total = total + ra[c, h, k].astype(F32)
             sb[c, h] = total.astype(BF16)
-        for k in (1, 2, 3):
-            out.append(remote(sb.at[c, 0, wrap(y, k)], rb.at[c, 0, k - 1], at_y(k)))
-            out.append(remote(sb.at[c, 1, wrap(x, k)], rb.at[c, 1, k - 1], at_x(k)))
-            out.append(remote(sq.at[c, 1], rsq.at[c, 1, k - 1], at_y(k)))
+            for k in (1, 2, 3):
+                if h == 0:
+                    out.append(remote(sb.at[c, 0, wrap(y, k)], rb.at[c, 0, k - 1], at_y(k)))
+                    out.append(remote(sq.at[c, 1], rsq.at[c, 1, k - 1], at_y(k)))
+                else:
+                    out.append(remote(sb.at[c, 1, wrap(x, k)], rb.at[c, 1, k - 1], at_x(k)))
         return out
 
     def queries(c, copies):
@@ -242,53 +253,51 @@
             jnp.concatenate([head[r * STEPS : (r + 1) * STEPS] for head in heads], axis=0)
             for r in range(RPC)
         ]
-        return rows, new_key, new_value
+        return jnp.concatenate(rows, axis=0).astype(BF16), new_key, new_value
 
     nq = GROUP * STEPS
 
-    def attention_scores(c, rows, new_key):
-        plain = jnp.concatenate(rows, axis=0).astype(BF16)
-        nothing = jnp.zeros_like(rows[0])
-        paired = jnp.concatenate(
-            [
-                jnp.concatenate([rows[0], nothing], axis=1),
-                jnp.concatenate([nothing, rows[1]], axis=1),
-            ],
-            axis=0,
-        ).astype(BF16)
+    def turn_keys(c):
+        for copy in load_kv[c]:
+            copy.wait()
+
+        @pl.loop(0, RPC * kbuf.shape[1] // TURN, unroll=2)
+        def _(n):
+            per_row = kbuf.shape[1] // TURN
+            r = c * RPC + n // per_row
+            where = pl.ds(pl.multiple_of(n % per_row * TURN, TURN), TURN)
+            kturned[r, :, where] = kbuf[r, where].T
+
+    def attention_scores(c, query, new_key):
         fresh = lax.dot_general(
-            plain, new_key, (((1,), (1,)), ((), ())), preferred_element_type=F32
-        )
-        query = iota(fresh.shape, 0)
+            query, new_key, (((1,), (1,)), ((), ())), preferred_element_type=F32
+        )
+        ask = iota(fresh.shape, 0)
         entry = iota(fresh.shape, 1)
-        allowed = (entry // STEPS == query // nq) & (entry % STEPS <= query % STEPS)
+        allowed = (entry // STEPS == ask // nq) & (entry % STEPS <= ask % STEPS)
         fresh = jnp.where(allowed, fresh, MASKED)
-        r = c * RPC
-        limits = (len_ref[r], len_ref[r + 1])
 
         def step(b, largest):
             start = pl.multiple_of(b * PBLK, PBLK)
             where = pl.ds(start, PBLK)
-            keys = jnp.concatenate([kbuf[r, where], kbuf[r + 1, where]], axis=1)
-            block = lax.dot_general(
-                paired, keys, (((1,), (1,)), ((), ())), preferred_element_type=F32
-            )
             place = iota((nq, PBLK), 1) + start
-            block = jnp.concatenate(
-                [
-                    jnp.where(place < limits[0], block[:nq], MASKED),
-                    jnp.where(place < limits[1], block[nq:], MASKED),
-                ],
-                axis=0,
-            )
-            scores[b] = block
-            for n in range(0, PBLK, HD):
-                largest = jnp.maximum(largest, block[:, n : n + HD])
-            return largest
-
-        largest = lax.fori_loop(
-            0, scores.shape[0], step, jnp.full((RPC * nq, HD), MASKED, F32), unroll=2
-        )
+            larger = []
+            for i in range(RPC):
+                own = slice(i * nq, (i + 1) * nq)
+                block = jnp.dot(
+                    query[own], kturned[c * RPC + i, :, where], preferred_element_type=F32
+                )
+                block = jnp.where(place < len_ref[c * RPC + i], block, MASKED)
+                scores[b, own] = block
+                top = largest[i]
+                for n in range(0, PBLK, HD):
+                    top = jnp.maximum(top, block[:, n : n + HD])
+                larger.append(top)
+            return tuple(larger)
+
+        least = jnp.full((nq, HD), MASKED, F32)
+        largest = lax.fori_loop(0, scores.shape[0], step, (least,) * RPC, unroll=2)
+        largest = jnp.concatenate(largest, axis=0)
         largest = jnp.maximum(
             jnp.max(largest, axis=1, keepdims=True), jnp.max(fresh, axis=1, keepdims=True)
         )
@@ -296,30 +305,36 @@
 
     def attention_values(c, state, new_value):
         allowed, fresh, largest = state
-        r = c * RPC
         fresh = jnp.where(allowed, jnp.exp(fresh - largest), 0.0)
         fresh_total = jnp.sum(fresh, axis=1, keepdims=True)
-        value = jnp.dot(fresh.astype(BF16), new_value, preferred_element_type=F32)
+        fresh_value = jnp.dot(fresh.astype(BF16), new_value, preferred_element_type=F32)
         level = jnp.broadcast_to(largest, (RPC * nq, HD))
 
         def step(b, state):
-            total, value = state
             where = pl.ds(pl.multiple_of(b * PBLK, PBLK), PBLK)
-            pieces = []
-            for n in range(0, PBLK, HD):
-                piece = jnp.exp(scores[b, :, n : n + HD] - level)
-                total = total + piece
-                pieces.append(piece.astype(BF16))
-            weights = jnp.concatenate(pieces, axis=1)
-            values = jnp.concatenate([vbuf[r, where], vbuf[r + 1, where]], axis=1)
-            value = value + jnp.dot(weights, values, preferred_element_type=F32)
-            return total, value
-
-        total, value = lax.fori_loop(
-            0, scores.shape[0], step,
-            (jnp.zeros((RPC * nq, HD), F32), jnp.concatenate([value, value], axis=1)), unroll=2,
-        )
-        return jnp.sum(total, axis=1, keepdims=True) + fresh_total, value
+            later = []
+            for i in range(RPC):
+                own = slice(i * nq, (i + 1) * nq)
+                total, value = state[i]
+                pieces = []
+                for n in range(0, PBLK, HD):
+                    piece = jnp.exp(scores[b, own, n : n + HD] - level[own])
+                    total = total + piece
+                    pieces.append(piece.astype(BF16))
+                weights = jnp.concatenate(pieces, axis=1)
+                value = value + jnp.dot(
+                    weights, vbuf[c * RPC + i, where], preferred_element_type=F32
+                )
+                later.append((total, value))
+            return tuple(later)
+
+        nothing = jnp.zeros((nq, HD), F32)
+        result = lax.fori_loop(
+            0, scores.shape[0], step, ((nothing, nothing),) * RPC, unroll=2
+        )
+        total = jnp.concatenate([total for total, _ in result], axis=0)
+        value = jnp.concatenate([value for _, value in result], axis=0)
+        return jnp.sum(total, axis=1, keepdims=True) + fresh_total, value + fresh_value
 
     def send_4a(c, state):
         total, value = state
@@ -328,7 +343,7 @@
         for g in range(GROUP):
             columns.append(jnp.concatenate(
                 [
-                    value[r * nq + g * STEPS : r * nq + (g + 1) * STEPS, r * HD : (r + 1) * HD]
+                    value[r * nq + g * STEPS : r * nq + (g + 1) * STEPS]
                     for r in range(RPC)
                 ],
                 axis=0,
@@ -387,33 +402,38 @@
             total = total + r5b[c, k].astype(F32)
         fin[pl.ds(c * SL, SL)] = total.astype(BF16).reshape(SL, total.shape[-1])
 
-    gather(0, True)
+    for b in range(nblk):
+        table_copies[b].wait()
+        if b == nblk - 1:
+            start_loads()
+        gather(0, b)
     pl.semaphore_wait(barrier, len(partners))
     a1 = send_1a(0)
-    gather(1, False)
+    for b in range(nblk // 2):
+        gather(1, b)
+    a1 = send_1b(0, a1)
+    for b in range(nblk // 2, nblk):
+        gather(1, b)
     b1 = send_1a(1)
-    a1 = send_1b(0, a1)
     b1 = send_1b(1, b1)
     a1 = send_1c(0, a1)
     b1 = send_1c(1, b1)
     a1 = send_1d(0, a1)
     load_w.wait()
+    a2 = send_2a(0, a1)
     b1 = send_1d(1, b1)
-    a2 = send_2a(0, a1)
     b2 = send_2a(1, b1)
+    turn_keys(0)
     a2 = send_2b(0, a2)
+    turn_keys(1)
     b2 = send_2b(1, b2)
     a_rows, a_key, a_value = queries(0, a2)
-    for copy in load_kv[0]:
-        copy.wait()
     state = attention_scores(0, a_rows, a_key)
     a4 = send_4a(0, attention_values(0, state, a_value))
     b_rows, b_key, b_value = queries(1, b2)
-    for copy in load_kv[1]:
-        copy.wait()
     state = attention_scores(1, b_rows, b_key)
+    b4 = send_4a(1, attention_values(1, state, b_value))
     a4 = send_4b(0, a4)
-    b4 = send_4a(1, attention_values(1, state, b_value))
     b4 = send_4b(1, b4)
 
     load_o.wait()
@@ -469,15 +489,19 @@
             jax.ShapeDtypeStruct((NCH * SL, out_cols), BF16),
             jax.ShapeDtypeStruct((NCH * TPD, 2 * HD), BF16),
         ),
-        in_specs=[vmem, smem, vmem, vmem, hbm, hbm, hbm, hbm, hbm],
+        in_specs=[smem] + [hbm] * 8,
         out_specs=(vmem, vmem),
         scratch_shapes=[
+            pltpu.VMEM(token_ids.shape, jnp.int32),
+            pltpu.VMEM(norm_gain.shape, BF16),
+            pltpu.VMEM(frequency.shape, F32),
             pltpu.VMEM((vocab // TBLK, TBLK, feats), BF16),
             pltpu.VMEM(qkv_weight.shape, BF16),
             pltpu.VMEM(out_weight.shape, BF16),
             pltpu.VMEM(key_cache.shape, BF16),
+            pltpu.VMEM((key_cache.shape[0], HD, key_cache.shape[1]), BF16),
             pltpu.VMEM(value_cache.shape, BF16),
-            pltpu.VMEM((TOK, feats), F32),
+            pltpu.VMEM((NCH, TOK, feats), F32),
             pltpu.VMEM((NCH, 4, 2, SL, feats), BF16),
             pltpu.VMEM((NCH, 4, SL, feats), BF16),
             pltpu.VMEM((NCH, 4, SL, feats), BF16),
@@ -495,6 +519,7 @@
             pltpu.VMEM((NCH, 4, 2, TPD, out_cols), BF16),
             pltpu.VMEM((NCH, 4, 2, TPD, out_cols), BF16),
             pltpu.VMEM((NCH, 3, 2, TPD, out_cols), BF16),
+            dma((3,)),
             dma((2 + 2 * NCH,)),
             dma((vocab // TBLK,)),
             dma((COPIES,)),
@@ -508,7 +533,7 @@
         ),
         name="decode_block",
     )(
-        token_ids, cache_lengths, norm_gain, jnp.asarray(frequency), embed_table,
+        cache_lengths, token_ids, norm_gain, jnp.asarray(frequency), embed_table,
         qkv_weight, key_cache, value_cache, out_weight,
     )
     out, kv = pl.pallas_call(

time: 61.5 us -> 58.1 us (0.945)
  Pallas kernels: 60.7 us -> 57.3 us
    pallas_call x1, Pallas kernels: 59 us -> 55.7 us  [body(): pl.pallas_call(kernel, out_shape=(jax.ShapeDtypeStruct((NCH * SL, out_col...]
where the time goes in v3:
time: 58.1 us; the launch traced here: 58 us
  Pallas kernels  57.3 us (99%)
  between operations  0.64 us (1%)
    pallas_call x1, Pallas kernels, body(): pl.pallas_call(kernel, out_shape=(jax.ShapeDtypeStruct((NCH * SL, out_col...  55.7 us
    pallas_call x1, Pallas kernels, body(): pl.pallas_call(order_outputs, out_shape=(jax.ShapeDtypeStruct((NCH * SL,...  1.64 us

profile of v3, /device:TPU:1, one launch (start us, length us, event | category | flops | bytes accessed | tf_op | source)
XLA Modules:
  0.0 58.0 jit_solution(15525694209122977528)
XLA Ops:
  0.6 55.7 %decode_block.1 = (bf16[64,512]{1,0:T(8,128)(2,1)}, bf16[32,256]{1,0:T(8,128)(2,1)}) custom-call(s32[4]{0:T(128)} %len_ref.1, s32[8,64]{1,0:T(8,128)} %ids_hbm.1, bf16[512]{0:T(512)(128)(2,1)} %gain_hbm.1, f32[1,128]{1,0:T(1,128)} %constant.2.clone.freq_hbm, bf16[8192,512]{1,0:T(8,128)(2,1)} %table_hbm.1, bf16[512,1280]{1,0:T(8,128)(2,1)} %wqkv_hbm.1, ...), custom_call_target="tpu_custom_call" | custom-call | flops 8000000000 | bytes 30000000 | tf_op jit(solution)/shard_map/decode_block/pallas_call | solution.py:486
  56.3 1.6 %order_outputs.1 = (bf16[64,512]{1,0:T(8,128)(2,1)}, bf16[2,32,128]{2,1,0:T(8,128)(2,1)}) custom-call(bf16[64,512]{1,0:T(8,128)(2,1)} %get-tuple-element.6.fin, bf16[32,256]{1,0:T(8,128)(2,1)} %get-tuple-element.7.kvs), custom_call_target="tpu_custom_call" | custom-call | tf_op jit(solution)/shard_map/order_outputs/pallas_call | solution.py:539

commit v4 on v3

v4 whole, which is shorter than its diff:
```python
import functools
import math

import jax
import jax.numpy as jnp
import numpy as np
from jax import lax
from jax.experimental import pallas as pl
from jax.experimental.pallas import tpu as pltpu
from jax.sharding import PartitionSpec as P

D = 8192
HD = 128
GROUP = 8
STEPS = 8
THETA = 500000.0
EPS = 1e-05
MASKED = -1e30
MESH = pl.DeviceIdType.MESH

ROWS = 4
CHUNKS = ((0, 2), (2, 1), (3, 1))
NGR = 2
PARTS = ((0,), (1, 2))
GTOK = 16 * 2 * STEPS
GSL = GTOK // 8
TBLK = 2048
PBLK = 4096
TURN = 1024
F32 = jnp.float32
BF16 = jnp.bfloat16


def iota(shape, dim):
    return lax.broadcasted_iota(jnp.int32, shape, dim)


def kernel(
    len_ref, ids_hbm, gain_hbm, freq_hbm, table_hbm, wqkv_hbm, key_hbm, val_hbm, wout_hbm,
    fin, kvs,
    ids_ref, gain_ref, freq_ref, table, wqkv, wout, kbuf, kturned, vbuf, acc,
    picks, r1a, s1, r1b, eall, scores, turn, chunks,
    small_sem, local_sem, table_sem, send_sem, recv_sem,
):
    gx = lax.axis_index("gx")
    gy = lax.axis_index("gy")
    z, core = gx // 2, gx % 2
    y, x = gy // 4, gy % 4

    def wrap(a, k):
        return (a + k) % 4

    def at_core():
        return (z * 2 + 1 - core, gy)

    def at_z(k):
        return (wrap(z, k) * 2 + core, gy)

    def at_y(k):
        return (gx, wrap(y, k) * 4 + x)

    def at_x(k):
        return (gx, y * 4 + wrap(x, k))

    counter = [0]
    sends = []

    def remote(src, dst, device):
        n = counter[0]
        counter[0] += 1
        copy = pltpu.make_async_remote_copy(
            src_ref=src, dst_ref=dst, send_sem=send_sem.at[n], recv_sem=recv_sem.at[n],
            device_id=device, device_id_type=MESH,
        )
        copy.start()
        sends.append(copy)
        return copy

    small = [
        pltpu.make_async_copy(hbm, ref, small_sem.at[n])
        for n, (hbm, ref) in enumerate(
            ((ids_hbm, ids_ref), (gain_hbm, gain_ref), (freq_hbm, freq_ref))
        )
    ]
    for copy in small:
        copy.start()
    nblk = table.shape[0]
    table_copies = []
    for b in range(nblk):
        copy = pltpu.make_async_copy(
            table_hbm.at[pl.ds(b * TBLK, TBLK)], table.at[b], table_sem.at[b]
        )
        copy.start()
        table_copies.append(copy)
    load_w = pltpu.make_async_copy(wqkv_hbm, wqkv, local_sem.at[0])
    load_o = pltpu.make_async_copy(wout_hbm, wout, local_sem.at[1])
    load_kv = []
    for first, rpc in CHUNKS:
        rows = pl.ds(first, rpc)
        c = len(load_kv)
        load_kv.append((
            pltpu.make_async_copy(key_hbm.at[rows], kbuf.at[rows], local_sem.at[2 + 2 * c]),
            pltpu.make_async_copy(val_hbm.at[rows], vbuf.at[rows], local_sem.at[3 + 2 * c]),
        ))

    def start_loads():
        load_w.start()
        for pair in load_kv:
            for copy in pair:
                copy.start()
        load_o.start()

    barrier = pltpu.get_barrier_semaphore()
    partners = [at_core()]
    for k in (1, 2, 3):
        partners += [at_z(k), at_y(k), at_x(k)]
    for device in partners:
        pl.semaphore_signal(barrier, inc=1, device_id=device, device_id_type=MESH)

    for copy in small:
        copy.wait()
    ids = ids_ref[...]
    id_high = (ids >> 8).astype(F32).astype(BF16)
    id_low = (ids & 255).astype(F32).astype(BF16)

    def local_ids(g):
        first, rpc = CHUNKS[PARTS[g][0]]
        token = iota((GTOK, 64), 0)
        place = token % (16 * rpc * STEPS)
        row = place // (rpc * STEPS) * ROWS + first
        row = row + token // (16 * rpc * STEPS) + place // STEPS % rpc
        chosen = jnp.where(iota((GTOK, 64), 1) == row, 1.0, 0.0).astype(BF16)
        contract = (((1,), (1,)), ((), ()))
        high = lax.dot_general(chosen, id_high, contract, preferred_element_type=F32)
        low = lax.dot_general(chosen, id_low, contract, preferred_element_type=F32)
        both = high * 256.0 + low
        mine = iota((GTOK, STEPS), 1) == iota((GTOK, STEPS), 0) % STEPS
        column = jnp.sum(jnp.where(mine, both, 0.0), axis=1, keepdims=True)
        return column.astype(jnp.int32) - gx * (nblk * TBLK)

    local = [local_ids(g) for g in range(NGR)]

    def gather(c, b):
        hot = jnp.where(iota((GTOK, TBLK), 1) == local[c] - b * TBLK, 1.0, 0.0).astype(BF16)
        term = jnp.dot(hot, table[b], preferred_element_type=F32)
        if b == 0:
            acc[c] = term
        elif b < nblk - 1:
            acc[c] += term
        else:
            picks[c] = (acc[c] + term).astype(BF16).reshape(picks.shape[1:])

    def send_1a(c):
        return remote(picks.at[c, :, 1 - core], r1a.at[c], at_core())

    def send_1b(c, copy):
        copy.wait_recv()
        s1[c] = picks[c, :, core] + r1a[c]
        return [remote(s1.at[c, wrap(z, k)], r1b.at[c, k - 1], at_z(k)) for k in (1, 2, 3)]

    def send_1c(c, copies):
        for copy in copies:
            copy.wait_recv()
        eall[c, z, core] = (s1[c, z] + r1b[c, 0]) + (r1b[c, 1] + r1b[c, 2])
        mine = eall.at[c, z, core]
        return (
            [remote(mine, mine, at_z(k)) for k in (1, 2, 3)],
            [remote(mine, mine, at_core())],
        )

    def send_1d(c, copies):
        across, over = copies
        for k, copy in zip((1, 2, 3), across):
            copy.wait_recv()
            block = eall.at[c, wrap(z, 4 - k), core]
            over.append(remote(block, block, at_core()))
        return over

    half = wqkv.shape[1] // 2

    def send_2a(c):
        rpc = CHUNKS[c][1]
        tok = 16 * rpc * STEPS
        g = 0 if c in PARTS[0] else 1
        size = 4 // len(PARTS[g])
        embedded = eall[g, pl.ds(PARTS[g].index(c) * size, size)]
        embedded = embedded.reshape(tok, eall.shape[-1]).astype(F32)
        scaled = (embedded * gain_ref[...].astype(F32)[None, :]).astype(BF16)
        out = []
        for h in range(2):
            own = pl.ds(h * half, half)
            product = jnp.dot(scaled, wqkv[:, own], preferred_element_type=F32)
            chunks[c]["part"][:, :, :, own] = product.astype(BF16).reshape(4, 4, rpc * STEPS, half)
            for k in (1, 2, 3):
                if h == 0:
                    block, device = chunks[c]["part"].at[:, wrap(x, k), :, own], at_x(k)
                else:
                    block, device = chunks[c]["part"].at[wrap(y, k), :, :, own], at_y(k)
                out.append(remote(block, chunks[c]["ra"].at[h, k - 1], device))
        squares = embedded * embedded
        high = squares.astype(BF16)
        low = (squares - high.astype(F32)).astype(BF16)
        ones = jnp.ones((8, eall.shape[-1]), BF16)
        contract = (((1,), (1,)), ((), ()))
        total = lax.dot_general(ones, high, contract, preferred_element_type=F32)
        total = total + lax.dot_general(ones, low, contract, preferred_element_type=F32)
        chunks[c]["sq"][0] = total[:1]
        for k in (1, 2, 3):
            out.append(remote(chunks[c]["sq"].at[0], chunks[c]["rsq"].at[0, k - 1], at_x(k)))
        return out

    def send_2b(c, copies):
        for copy in copies:
            copy.wait_recv()
        chunks[c]["sq"][1] = (chunks[c]["sq"][0] + chunks[c]["rsq"][0, 0]) + (chunks[c]["rsq"][0, 1] + chunks[c]["rsq"][0, 2])
        out = []
        for h, own in ((0, chunks[c]["part"][:, x, :, pl.ds(0, half)]), (1, chunks[c]["part"][y, :, :, pl.ds(half, half)])):
            total = own.astype(F32)
            for k in range(3):
                total = total + chunks[c]["ra"][h, k].astype(F32)
            chunks[c]["sb"][h] = total.astype(BF16)
            for k in (1, 2, 3):
                if h == 0:
                    out.append(remote(chunks[c]["sb"].at[0, wrap(y, k)], chunks[c]["rb"].at[0, k - 1], at_y(k)))
                    out.append(remote(chunks[c]["sq"].at[1], chunks[c]["rsq"].at[1, k - 1], at_y(k)))
                else:
                    out.append(remote(chunks[c]["sb"].at[1, wrap(x, k)], chunks[c]["rb"].at[1, k - 1], at_x(k)))
        return out

    def rotary():
        entry = iota((ROWS * STEPS, 1), 0)
        length = jnp.zeros_like(entry)
        for r in range(ROWS):
            length = jnp.where(entry // STEPS == r, len_ref[r], length)
        angle = (length + entry % STEPS).astype(F32) * freq_ref[...]
        sine = jnp.sin(angle)
        turn[0] = jnp.cos(angle)
        turn[1] = jnp.where(iota(sine.shape, 1) < HD // 2, -sine, sine)

    def queries(c, copies):
        first, rpc = CHUNKS[c]
        tpd = rpc * STEPS
        tok = 16 * tpd
        for copy in copies:
            copy.wait_recv()
        squares = (chunks[c]["sq"][1] + chunks[c]["rsq"][1, 0]) + (chunks[c]["rsq"][1, 1] + chunks[c]["rsq"][1, 2])
        place = iota((tpd, tok), 1) == iota((tpd, tok), 0) + gy * tpd
        column = jnp.sum(jnp.where(place, squares, 0.0), axis=1, keepdims=True)
        inverse_rms = lax.rsqrt(column / D + EPS)
        pieces = []
        for h, own in ((0, chunks[c]["sb"][0, y]), (1, chunks[c]["sb"][1, x])):
            total = own.astype(F32)
            for k in range(3):
                total = total + chunks[c]["rb"][h, k].astype(F32)
            pieces.append(total)
        projected = jnp.concatenate(pieces, axis=1) * inverse_rms
        own = pl.ds(first * STEPS, tpd)
        cosine, sine = turn[0, own], turn[1, own]

        def rotate(g):
            field = projected[:, g * HD : (g + 1) * HD]
            return field * cosine + pltpu.roll(field, HD // 2, 1) * sine

        heads = [rotate(g) * HD ** (-0.5) for g in range(GROUP)]
        new_key = rotate(GROUP).astype(BF16)
        new_value = projected[:, (GROUP + 1) * HD :].astype(BF16)
        fresh = jnp.concatenate([new_key, new_value], axis=1)
        kvs[pl.ds(first * STEPS, tpd)] = fresh.astype(F32)
        rows = [
            jnp.concatenate([head[r * STEPS : (r + 1) * STEPS] for head in heads], axis=0)
            for r in range(rpc)
        ]
        return jnp.concatenate(rows, axis=0).astype(BF16), new_key, new_value

    nq = GROUP * STEPS

    def turn_keys(c):
        first, rpc = CHUNKS[c]
        for copy in load_kv[c]:
            copy.wait()

        @pl.loop(0, rpc * kbuf.shape[1] // TURN, unroll=2)
        def _(n):
            per_row = kbuf.shape[1] // TURN
            r = first + n // per_row
            where = pl.ds(pl.multiple_of(n % per_row * TURN, TURN), TURN)
            kturned[r, :, where] = kbuf[r, where].T

    def attention_scores(c, query, new_key):
        first, rpc = CHUNKS[c]
        fresh = lax.dot_general(
            query, new_key, (((1,), (1,)), ((), ())), preferred_element_type=F32
        )
        ask = iota(fresh.shape, 0)
        entry = iota(fresh.shape, 1)
        allowed = (entry // STEPS == ask // nq) & (entry % STEPS <= ask % STEPS)
        fresh = jnp.where(allowed, fresh, MASKED)

        def step(b, largest):
            start = pl.multiple_of(b * PBLK, PBLK)
            where = pl.ds(start, PBLK)
            place = iota((nq, PBLK), 1) + start
            larger = []
            for i in range(rpc):
                own = slice(i * nq, (i + 1) * nq)
                block = jnp.dot(
                    query[own], kturned[first + i, :, where], preferred_element_type=F32
                )
                block = jnp.where(place < len_ref[first + i], block, MASKED)
                scores[b, own] = block
                top = largest[i]
                for n in range(0, PBLK, HD):
                    top = jnp.maximum(top, block[:, n : n + HD])
                larger.append(top)
            return tuple(larger)

        least = jnp.full((nq, HD), MASKED, F32)
        largest = lax.fori_loop(0, scores.shape[0], step, (least,) * rpc, unroll=2)
        largest = jnp.concatenate(largest, axis=0)
        largest = jnp.maximum(
            jnp.max(largest, axis=1, keepdims=True), jnp.max(fresh, axis=1, keepdims=True)
        )
        return allowed, fresh, largest

    def attention_values(c, state, new_value):
        first, rpc = CHUNKS[c]
        allowed, fresh, largest = state
        fresh = jnp.where(allowed, jnp.exp(fresh - largest), 0.0)
        fresh_total = jnp.sum(fresh, axis=1, keepdims=True)
        fresh_value = jnp.dot(fresh.astype(BF16), new_value, preferred_element_type=F32)
        level = jnp.broadcast_to(largest, (rpc * nq, HD))

        def step(b, state):
            where = pl.ds(pl.multiple_of(b * PBLK, PBLK), PBLK)
            later = []
            for i in range(rpc):
                own = slice(i * nq, (i + 1) * nq)
                total, value = state[i]
                pieces = []
                for n in range(0, PBLK, HD):
                    piece = jnp.exp(scores[b, own, n : n + HD] - level[own])
                    total = total + piece
                    pieces.append(piece.astype(BF16))
                weights = jnp.concatenate(pieces, axis=1)
                value = value + jnp.dot(
                    weights, vbuf[first + i, where], preferred_element_type=F32
                )
                later.append((total, value))
            return tuple(later)

        nothing = jnp.zeros((nq, HD), F32)
        result = lax.fori_loop(
            0, scores.shape[0], step, ((nothing, nothing),) * rpc, unroll=2
        )
        total = jnp.concatenate([total for total, _ in result], axis=0)
        value = jnp.concatenate([value for _, value in result], axis=0)
        return jnp.sum(total, axis=1, keepdims=True) + fresh_total, value + fresh_value

    def send_4a(c, state):
        rpc = CHUNKS[c][1]
        total, value = state
        value = value / total
        columns = []
        for g in range(GROUP):
            columns.append(jnp.concatenate(
                [
                    value[r * nq + g * STEPS : r * nq + (g + 1) * STEPS]
                    for r in range(rpc)
                ],
                axis=0,
            ))
        chunks[c]["ag"][0, 0] = jnp.concatenate(columns, axis=1).astype(BF16)
        own = chunks[c]["ag"].at[0, 0]
        out = ([], [])
        for k in (1, 2, 3):
            out[0].append(remote(own, chunks[c]["ag"].at[0, k], at_x(k)))
            out[1].append(remote(own, chunks[c]["ag"].at[k, 0], at_y(k)))
        return out

    ahalf = wout.shape[0] // 2

    def send_4b(c, copies):
        along_x, along_y = copies
        out = []
        left, right = pl.ds(0, ahalf), pl.ds(ahalf, ahalf)
        others = pl.ds(1, 3)
        for copy in along_x:
            copy.wait_recv()
        for k in (1, 2, 3):
            out.append(remote(
                chunks[c]["ag"].at[0, others, :, left], chunks[c]["ag"].at[k, others, :, left], at_y(k)
            ))
        for copy in along_y:
            copy.wait_recv()
        for k in (1, 2, 3):
            out.append(remote(
                chunks[c]["ag"].at[others, 0, :, right], chunks[c]["ag"].at[others, k, :, right], at_x(k)
            ))
        return out

    def send_5a(c, copies):
        for copy in copies:
            copy.wait_recv()
        tpd = CHUNKS[c][1] * STEPS
        everyone = chunks[c]["ag"][...].reshape(16 * tpd, wout.shape[0])
        product = jnp.dot(everyone, wout[...], preferred_element_type=F32).astype(BF16)
        for ky in range(4):
            for kx in range(4):
                n = (ky * 4 + kx) * tpd
                place = wrap(x, 4 - kx)
                chunks[c]["part5"][wrap(y, 4 - ky), place // 2, place % 2] = product[n : n + tpd]
        return remote(chunks[c]["part5"].at[:, 1 - core], chunks[c]["r5a"], at_core())

    def send_5b(c, copy):
        copy.wait_recv()
        chunks[c]["s5"][...] = (chunks[c]["part5"][:, core].astype(F32) + chunks[c]["r5a"][...].astype(F32)).astype(BF16)
        return [remote(chunks[c]["s5"].at[wrap(z, k)], chunks[c]["r5b"].at[k - 1], at_z(k)) for k in (1, 2, 3)]

    def finish(c, copies):
        for copy in copies:
            copy.wait_recv()
        total = chunks[c]["s5"][z].astype(F32)
        for k in range(3):
            total = total + chunks[c]["r5b"][k].astype(F32)
        first, rpc = CHUNKS[c]
        size = 2 * rpc * STEPS
        fin[pl.ds(2 * first * STEPS, size)] = total.astype(BF16).reshape(size, total.shape[-1])

    for b in range(nblk):
        table_copies[b].wait()
        if b == nblk - 1:
            start_loads()
        gather(0, b)
    pl.semaphore_wait(barrier, len(partners))
    a1 = send_1a(0)
    for b in range(nblk // 2):
        gather(1, b)
    a1 = send_1b(0, a1)
    for b in range(nblk // 2, nblk):
        gather(1, b)
    b1 = send_1a(1)
    b1 = send_1b(1, b1)
    a1 = send_1c(0, a1)
    b1 = send_1c(1, b1)
    a1 = send_1d(0, a1)
    load_w.wait()
    for copy in a1:
        copy.wait_recv()
    p2 = [send_2a(0)]
    b1 = send_1d(1, b1)
    for copy in b1:
        copy.wait_recv()
    p2 += [send_2a(1), send_2a(2)]
    turn_keys(0)
    rotary()
    p2[0] = send_2b(0, p2[0])
    turn_keys(1)
    turn_keys(2)
    p2[1] = send_2b(1, p2[1])
    p4 = []
    query, new_key, new_value = queries(0, p2[0])
    state = attention_scores(0, query, new_key)
    p2[2] = send_2b(2, p2[2])
    p4.append(send_4a(0, attention_values(0, state, new_value)))
    for c in (1, 2):
        query, new_key, new_value = queries(c, p2[c])
        state = attention_scores(c, query, new_key)
        p4.append(send_4a(c, attention_values(c, state, new_value)))
    load_o.wait()
    p4[0] = send_4b(0, p4[0])
    p4[1] = send_4b(1, p4[1])
    p4[2] = send_4b(2, p4[2])
    p5 = [send_5a(0, p4[0])]
    p5.append(send_5a(1, p4[1]))
    p5[0] = send_5b(0, p5[0])
    p5.append(send_5a(2, p4[2]))
    p5[1] = send_5b(1, p5[1])
    p5[2] = send_5b(2, p5[2])
    for copy in sends:
        copy.wait_send()
    for c in range(len(CHUNKS)):
        finish(c, p5[c])


def order_outputs(fin, kvs, out_ref, kv_ref):
    size = ROWS * STEPS
    order = iota((size, size), 0)
    source = order % ROWS * STEPS + order // ROWS
    perm = jnp.where(iota((size, size), 1) == source, 1.0, 0.0).astype(BF16)
    fresh = jnp.dot(perm, kvs[...].astype(BF16), preferred_element_type=F32).astype(BF16)
    kv_ref[0] = fresh[:, :HD]
    kv_ref[1] = fresh[:, HD:]

    size = 2 * ROWS * STEPS
    order = iota((size, size), 0)
    step, side, row = order // (2 * ROWS), order // ROWS % 2, order % ROWS
    source = order
    for first, rpc in CHUNKS:
        inside = (row >= first) & (row < first + rpc)
        place = 2 * first * STEPS + side * rpc * STEPS + (row - first) * STEPS + step
        source = jnp.where(inside, place, source)
    perm = jnp.where(iota((size, size), 1) == source, 1.0, 0.0).astype(BF16)
    out_ref[...] = jnp.dot(perm, fin[...], preferred_element_type=F32).astype(BF16)


COPIES = NGR * (1 + 3 + 3 + 4) + len(CHUNKS) * (9 + 9 + 6 + 6 + 1 + 3)


def chunk_scratch(rows, cols, width, out_cols):
    tpd = rows * STEPS
    tok = 16 * tpd
    half = cols // 2
    return {
        "part": pltpu.VMEM((4, 4, tpd, cols), BF16),
        "ra": pltpu.VMEM((2, 3, 4, tpd, half), BF16),
        "sb": pltpu.VMEM((2, 4, tpd, half), BF16),
        "rb": pltpu.VMEM((2, 3, tpd, half), BF16),
        "sq": pltpu.VMEM((2, 1, tok), F32),
        "rsq": pltpu.VMEM((2, 3, 1, tok), F32),
        "ag": pltpu.VMEM((4, 4, tpd, width), BF16),
        "part5": pltpu.VMEM((4, 2, 2, tpd, out_cols), BF16),
        "r5a": pltpu.VMEM((4, 2, tpd, out_cols), BF16),
        "s5": pltpu.VMEM((4, 2, tpd, out_cols), BF16),
        "r5b": pltpu.VMEM((3, 2, tpd, out_cols), BF16),
    }


def body(
    token_ids, cache_lengths, embed_table, norm_gain, qkv_weight, key_cache, value_cache, out_weight
):
    vocab, feats = embed_table.shape
    cols = qkv_weight.shape[1]
    width, out_cols = out_weight.shape
    frequency = THETA ** (-np.arange(HD // 2, dtype=np.float64) * (2.0 / HD))
    frequency = np.concatenate([frequency, frequency]).astype(np.float32)[None, :]
    vmem = pl.BlockSpec(memory_space=pltpu.VMEM)
    hbm = pl.BlockSpec(memory_space=pl.ANY)
    smem = pl.BlockSpec(memory_space=pltpu.SMEM)
    dma = pltpu.SemaphoreType.DMA
    fin, kvs = pl.pallas_call(
        kernel,
        out_shape=(
            jax.ShapeDtypeStruct((2 * ROWS * STEPS, out_cols), BF16),
            jax.ShapeDtypeStruct((ROWS * STEPS, 2 * HD), F32),
        ),
        in_specs=[smem] + [hbm] * 8,
        out_specs=(vmem, vmem),
        scratch_shapes=[
            pltpu.VMEM(token_ids.shape, jnp.int32),
            pltpu.VMEM(norm_gain.shape, BF16),
            pltpu.VMEM(frequency.shape, F32),
            pltpu.VMEM((vocab // TBLK, TBLK, feats), BF16),
            pltpu.VMEM(qkv_weight.shape, BF16),
            pltpu.VMEM(out_weight.shape, BF16),
            pltpu.VMEM(key_cache.shape, BF16),
            pltpu.VMEM((key_cache.shape[0], HD, key_cache.shape[1]), BF16),
            pltpu.VMEM(value_cache.shape, BF16),
            pltpu.VMEM((NGR, GTOK, feats), F32),
            pltpu.VMEM((NGR, 4, 2, GSL, feats), BF16),
            pltpu.VMEM((NGR, 4, GSL, feats), BF16),
            pltpu.VMEM((NGR, 4, GSL, feats), BF16),
            pltpu.VMEM((NGR, 3, GSL, feats), BF16),
            pltpu.VMEM((NGR, 4, 2, GSL, feats), BF16),
            pltpu.VMEM((key_cache.shape[1] // PBLK, 2 * GROUP * STEPS, PBLK), F32),
            pltpu.VMEM((2, ROWS * STEPS, HD), F32),
            [chunk_scratch(rows, cols, width, out_cols) for _, rows in CHUNKS],
            dma((3,)),
            dma((2 + 2 * len(CHUNKS),)),
            dma((vocab // TBLK,)),
            dma((COPIES,)),
            dma((COPIES,)),
        ],
        compiler_params=pltpu.CompilerParams(
            collective_id=0, has_side_effects=True, vmem_limit_bytes=56 << 20
        ),
        cost_estimate=pl.CostEstimate(
            flops=8 * 10**9, bytes_accessed=30 * 10**6, transcendentals=2 * 10**6
        ),
        name="decode_block",
    )(
        cache_lengths, token_ids, norm_gain, jnp.asarray(frequency), embed_table,
        qkv_weight, key_cache, value_cache, out_weight,
    )
    out, kv = pl.pallas_call(
        order_outputs,
        out_shape=(
            jax.ShapeDtypeStruct((2 * ROWS * STEPS, out_cols), BF16),
            jax.ShapeDtypeStruct((2, ROWS * STEPS, HD), BF16),
        ),
        in_specs=[vmem, vmem],
        out_specs=(vmem, vmem),
        name="order_outputs",
    )(fin, kvs)
    return (
        out.reshape(STEPS, 2 * ROWS, out_cols),
        kv.reshape(2, STEPS, ROWS, HD),
    )


def solution(mesh):
    in_specs = (
        P(),
        P("gy"),
        P("gx", "gy"),
        P("gy"),
        P("gy", "gx"),
        P("gy", None, "gx"),
        P("gy", None, "gx"),
        P("gx", "gy"),
    )
    out_specs = (P(None, "gx", "gy"), P(None, None, "gy", "gx"))
    return jax.shard_map(body, mesh=mesh, in_specs=in_specs, out_specs=out_specs, check_vma=False)
```

time: 58.1 us -> 57.8 us (level)
  no operation moved by 1% of the time
where the time goes in v4:
time: 57.8 us; the launch traced here: 57.6 us
  Pallas kernels  57 us (99%)
  between operations  0.64 us (1%)
    pallas_call x1, Pallas kernels, body(): pl.pallas_call(kernel, out_shape=(jax.ShapeDtypeStruct((2 * ROWS * STEPS,...  55.4 us
    pallas_call x1, Pallas kernels, body(): pl.pallas_call(order_outputs, out_shape=(jax.ShapeDtypeStruct((2 * ROWS *...  1.64 us

profile of v4, /device:TPU:1, one launch (start us, length us, event | category | flops | bytes accessed | tf_op | source)
XLA Modules:
  0.0 57.6 jit_solution(9817405399916045754)
XLA Ops:
  0.6 55.4 %decode_block.1 = (bf16[64,512]{1,0:T(8,128)(2,1)}, f32[32,256]{1,0:T(8,128)}) custom-call(s32[4]{0:T(128)} %len_ref.1, s32[8,64]{1,0:T(8,128)} %ids_hbm.1, bf16[512]{0:T(512)(128)(2,1)} %gain_hbm.1, f32[1,128]{1,0:T(1,128)} %constant.2.clone.freq_hbm, bf16[8192,512]{1,0:T(8,128)(2,1)} %table_hbm.1, bf16[512,1280]{1,0:T(8,128)(2,1)} %wqkv_hbm.1, ...), custom_call_target="tpu_custom_call" | custom-call | flops 8000000000 | bytes 30000000 | tf_op jit(solution)/shard_map/decode_block/pallas_call | solution.py:540
  56.0 1.6 %order_outputs.1 = (bf16[64,512]{1,0:T(8,128)(2,1)}, bf16[2,32,128]{2,1,0:T(8,128)(2,1)}) custom-call(bf16[64,512]{1,0:T(8,128)(2,1)} %get-tuple-element.6.fin, f32[32,256]{1,0:T(8,128)} %get-tuple-element.7.kvs), custom_call_target="tpu_custom_call" | custom-call | tf_op jit(solution)/shard_map/order_outputs/pallas_call | solution.py:584

commit v5 on v4

--- a/solution.py
+++ b/solution.py
@@ -197,6 +197,14 @@
                 else:
                     block, device = chunks[c]["part"].at[wrap(y, k), :, :, own], at_y(k)
                 out.append(remote(block, chunks[c]["ra"].at[h, k - 1], device))
+        return out
+
+    def send_squares(c):
+        g = 0 if c in PARTS[0] else 1
+        size = 4 // len(PARTS[g])
+        embedded = eall[g, pl.ds(PARTS[g].index(c) * size, size)]
+        embedded = embedded.reshape(16 * CHUNKS[c][1] * STEPS, eall.shape[-1]).astype(F32)
+        out = []
         squares = embedded * embedded
         high = squares.astype(BF16)
         low = (squares - high.astype(F32)).astype(BF16)
@@ -447,10 +455,13 @@
     for copy in a1:
         copy.wait_recv()
     p2 = [send_2a(0)]
+    p2[0] += send_squares(0)
     b1 = send_1d(1, b1)
     for copy in b1:
         copy.wait_recv()
     p2 += [send_2a(1), send_2a(2)]
+    p2[1] += send_squares(1)
+    p2[2] += send_squares(2)
     turn_keys(0)
     rotary()
     p2[0] = send_2b(0, p2[0])

time: 57.8 us -> 57.2 us (0.990)
  Pallas kernels: 57 us -> 56.4 us
    pallas_call x1, Pallas kernels: 55.4 us -> 54.8 us  [body(): pl.pallas_call(kernel, out_shape=(jax.ShapeDtypeStruct((2 * ROWS * STEPS,...]
where the time goes in v5:
time: 57.2 us; the launch traced here: 57 us
  Pallas kernels  56.4 us (99%)
  between operations  0.64 us (1%)
    pallas_call x1, Pallas kernels, body(): pl.pallas_call(kernel, out_shape=(jax.ShapeDtypeStruct((2 * ROWS * STEPS,...  54.8 us
    pallas_call x1, Pallas kernels, body(): pl.pallas_call(order_outputs, out_shape=(jax.ShapeDtypeStruct((2 * ROWS *...  1.64 us

profile of v5, /device:TPU:1, one launch (start us, length us, event | category | flops | bytes accessed | tf_op | source)
XLA Modules:
  0.0 57.0 jit_solution(11994842433270191708)
XLA Ops:
  0.6 54.8 %decode_block.1 = (bf16[64,512]{1,0:T(8,128)(2,1)}, f32[32,256]{1,0:T(8,128)}) custom-call(s32[4]{0:T(128)} %len_ref.1, s32[8,64]{1,0:T(8,128)} %ids_hbm.1, bf16[512]{0:T(512)(128)(2,1)} %gain_hbm.1, f32[1,128]{1,0:T(1,128)} %constant.2.clone.freq_hbm, bf16[8192,512]{1,0:T(8,128)(2,1)} %table_hbm.1, bf16[512,1280]{1,0:T(8,128)(2,1)} %wqkv_hbm.1, ...), custom_call_target="tpu_custom_call" | custom-call | flops 8000000000 | bytes 30000000 | tf_op jit(solution)/shard_map/decode_block/pallas_call | solution.py:551
  55.4 1.6 %order_outputs.1 = (bf16[64,512]{1,0:T(8,128)(2,1)}, bf16[2,32,128]{2,1,0:T(8,128)(2,1)}) custom-call(bf16[64,512]{1,0:T(8,128)(2,1)} %get-tuple-element.6.fin, f32[32,256]{1,0:T(8,128)} %get-tuple-element.7.kvs), custom_call_target="tpu_custom_call" | custom-call | tf_op jit(solution)/shard_map/order_outputs/pallas_call | solution.py:595
